TPU v7x, 256 devices: a whole 4x4x8 slice. The times are simulated.
256 devices in a mesh: dp: 16 (over y, x), mp: 16 (over z, core).
Axes of the slice: x: 4, y: 4, z: 8, core: 2. Of those that a mesh axis runs over, the one named last changes fastest.
Arguments:
- features: bfloat16 [2, 1536, 8192], P(None, 'dp'), as said below
- weight: bfloat16 [8192, 8192], P(None, 'mp'), may hold values from -0.0625 to 0.0625
Outputs:
- grad_weight: float32 [8192, 8192], P('dp', 'mp')
- loss_value: float32 [], replicated
Inputs may be any that keep to these rules, and one draw needn't show every extreme that they name: Nonnegative post-activation features.
All inputs are finite; a program needn't handle non-finite values.
Results may differ from a plain program's by a relative error of at most 0.0016.
Values may be sent and summed in bfloat16 or wider, within the bound.
A program may use at most 128 MiB of HBM per device.

v0:
```python
import jax
import jax.numpy as jnp
from jax import lax
from jax.sharding import PartitionSpec as P

epsilon = 1e-05
off_weight = 0.0051


def body(features, weight):
    row_count = features.shape[1]
    full_width = features.shape[2]
    col_count = weight.shape[1]
    batch_size = row_count * lax.axis_size("dp")
    block_rows = full_width // lax.axis_size("dp")
    projected = jnp.einsum("vrk,kc->vrc", features, weight, preferred_element_type=jnp.float32)
    sum_first = lax.psum(jnp.sum(projected, axis=1), "dp")
    moment_mean = sum_first / batch_size
    shifted = projected - moment_mean[:, None, :]
    spread = lax.psum(jnp.sum(shifted * shifted, axis=1), "dp")
    variance = spread / batch_size
    inv_std = lax.rsqrt(variance + epsilon)
    centered = shifted * inv_std[:, None, :]
    normed = centered.astype(jnp.bfloat16)
    first_full = lax.all_gather(normed[0], "mp", axis=1, tiled=True)
    first_block = lax.all_to_all(first_full, "dp", split_axis=1, concat_axis=0, tiled=True)
    second_cols = lax.all_gather(normed[1], "dp", axis=0, tiled=True)
    correlation = (
        lax.dot_general(
            first_block, second_cols, (((0,), (0,)), ((), ())), preferred_element_type=jnp.float32
        )
        / batch_size
    )
    row_ids = lax.axis_index("dp") * block_rows + lax.broadcasted_iota(
        jnp.int32, (block_rows, col_count), 0
    )
    col_ids = lax.axis_index("mp") * col_count + lax.broadcasted_iota(
        jnp.int32, (block_rows, col_count), 1
    )
    on_diagonal = row_ids == col_ids
    terms = jnp.where(on_diagonal, (1.0 - correlation) ** 2, off_weight * correlation * correlation)
    loss_value = lax.psum(jnp.sum(terms), ("dp", "mp")) / full_width
    corr_grad = jnp.where(
        on_diagonal, 2.0 * (correlation - 1.0), 2.0 * off_weight * correlation
    ).astype(jnp.bfloat16)
    second_local = normed[1]
    incoming = lax.all_gather(corr_grad, "dp", axis=0, tiled=True)
    across = lax.dot_general(
        second_local, incoming, (((1,), (1,)), ((), ())), preferred_element_type=jnp.float32
    )
    second_part = jnp.dot(first_full, incoming, preferred_element_type=jnp.float32)
    grad_first = lax.psum_scatter(across, "mp", scatter_dimension=1, tiled=True) / batch_size
    grad_second = second_part / batch_size
    normed_grad = jnp.stack([grad_first, grad_second])
    grad_sum, cross_sum = lax.psum(
        (jnp.sum(normed_grad, axis=1), jnp.sum(normed_grad * centered, axis=1)), "dp"
    )
    out_grad = (
        inv_std[:, None, :]
        * (
            normed_grad
            - grad_sum[:, None, :] / batch_size
            - centered * (cross_sum[:, None, :] / batch_size)
        )
    ).astype(jnp.bfloat16)
    grad_weight = lax.psum_scatter(
        jnp.einsum("vrk,vrc->kc", features, out_grad, preferred_element_type=jnp.float32),
        "dp",
        scatter_dimension=0,
        tiled=True,
    )
    return (grad_weight, loss_value)


def solution(mesh):
    placed = (P(None, "dp", None), P(None, "mp"))
    return jax.shard_map(
        body, mesh=mesh, in_specs=placed, out_specs=(P("dp", "mp"), P()), check_vma=False
    )
```

profile of v0, /device:TPU:2, one launch (start us, length us, event | category | flops | bytes accessed | tf_op | source)
XLA Modules:
  0.0 512.5 jit_solution(6534553959964706231)
XLA Ops:
  7.2 1.8 copy-done
  9.1 5.2 %fusion.26 = (f32[2,512]{1,0:T(2,128)S(1)}, f32[2,96,512]{2,1,0:T(8,128)S(1)}) fusion(bf16[2,96,8192]{2,1,0:T(8,128)(2,1)S(1)} %copy-done, bf16[8192,512]{1,0:T(8,128)(2,1)} %param.3), kind=kOutput, calls=%fused_computation.38 | convolution fusion | flops 1610710016 | bytes 11931648 | tf_op jit(solution)/shard_map/vrk,kc->vrc/dot_general | solution.py:16
  14.2 37.7 %psum.35 = f32[2,512]{1,0:T(2,128)S(1)} all-reduce(f32[2,512]{1,0:T(2,128)S(1)} %get-tuple-element.14), channel_id=1, replica_groups=mesh['dp'=16,'mp'=16] {'dp'}, use_global_device_ids=true, to_apply=%region_1.0 | all-reduce | flops 1024 | bytes 8192 | tf_op jit(solution)/shard_map/psum | solution.py:17
  52.0 38.9 %psum.36 = f32[2,512]{1,0:T(2,128)S(1)} all-reduce(f32[2,512]{1,0:T(2,128)S(1)} %multiply_reduce_fusion.1), channel_id=1, replica_groups=mesh['dp'=16,'mp'=16] {'dp'}, use_global_device_ids=true, to_apply=%region_3.0 | all-reduce | flops 1024 | bytes 8192 | tf_op jit(solution)/shard_map/psum | solution.py:20
  91.0 0.7 copy-done.2
  92.5 0.7 all-gather.10.cloned.1.call-update
  93.2 37.3 %all-gather.8.cloned.1.call-done = bf16[1,96,8192]{2,1,0:T(8,128)(2,1)} async-done(((bf16[1,96,512]{2,1,0:T(8,128)(2,1)}), bf16[1,96,8192]{2,1,0:T(8,128)(2,1)}) %all-gather.8.cloned.1.call-update) | async-done | bytes 1572880 | tf_op jit(solution)/shard_map/all_gather | solution.py:25
  130.5 2.0 copy.7
  132.5 2.0 copy.5
  134.5 7.3 %all-to-all-start = ((bf16[96,16,512]{2,0,1:T(8,128)(2,1)}), bf16[96,16,512]{2,0,1:T(8,128)(2,1)}, u32[]{:S(2)}, u32[]{:S(2)}) async-start(bf16[96,16,512]{2,0,1:T(8,128)(2,1)} %copy.5), calls=%async_computation | async-start | bytes 3145728 | tf_op jit(solution)/shard_map/all_to_all | solution.py:26
  141.8 47.0 %all-gather.10.cloned.1.call-done = bf16[1,1536,512]{2,1,0:T(8,128)(2,1)} async-done(((bf16[1,96,512]{2,1,0:T(8,128)(2,1)}), bf16[1,1536,512]{2,1,0:T(8,128)(2,1)}) %all-gather.10.cloned.1.call-update) | async-done | bytes 1572880 | tf_op jit(solution)/shard_map/all_gather | solution.py:27
  188.8 4.6 fusion.13
  193.4 75.7 %all-gather.6.cloned.1.call-done = bf16[8192,512]{1,0:T(8,128)(2,1)} async-done(((bf16[512,512]{1,0:T(8,128)(2,1)}), bf16[8192,512]{1,0:T(8,128)(2,1)}) %all-gather.6.cloned.1.call-update) | async-done | bytes 8388624 | tf_op jit(solution)/shard_map/all_gather | solution.py:47
  269.1 7.8 %fusion.21 = f32[96,8192]{1,0:T(8,128)} fusion(bf16[8192,512]{1,0:T(8,128)(2,1)} %all-gather.6.cloned.1.call-done, bf16[2,96,512]{2,1,0:T(8,128)(2,1)} %copy-done.2), kind=kOutput, calls=%fused_computation.27 | convolution fusion | flops 805306368 | bytes 11632640 | tf_op jit(solution)/shard_map/dot_general | solution.py:48
  277.0 6.0 %fusion.9 = f32[1,96,512]{2,1,0:T(8,128)} fusion(bf16[8192,512]{1,0:T(8,128)(2,1)} %all-gather.6.cloned.1.call-done, bf16[1,96,8192]{2,1,0:T(8,128)(2,1)} %all-gather.8.cloned.1.call-done), kind=kOutput, calls=%fused_computation.10 | convolution fusion | flops 805355520 | bytes 10158080 | tf_op jit(solution)/shard_map/dot_general | solution.py:51
  283.0 54.8 %reduce-scatter.3.cloned.1.call-done = f32[96,512]{1,0:T(8,128)} async-done(((f32[96,8192]{1,0:T(8,128)}), f32[96,512]{1,0:T(8,128)}) %reduce-scatter.3.cloned.1.call-update) | async-done | bytes 196624 | tf_op jit(solution)/shard_map/reduce_scatter | solution.py:52
  337.8 0.9 multiply_bitcast_fusion
  339.5 1.0 fusion.16
  340.5 37.3 %all-reduce = (f32[2,512]{1,0:T(2,128)}, f32[2,512]{1,0:T(2,128)}) all-reduce(f32[2,512]{1,0:T(2,128)S(1)} %get-tuple-element.7, f32[2,512]{1,0:T(2,128)S(1)} %get-tuple-element.6), channel_id=1, replica_groups=mesh['dp'=16,'mp'=16] {'dp'}, use_global_device_ids=true, to_apply=%region_8.9 | all-reduce | flops 2048 | bytes 16384 | tf_op jit(solution)/shard_map/psum | solution.py:55
  377.8 0.7 broadcast_multiply_fusion
  379.1 9.1 %convolution_bitcast_fusion = f32[8192,512]{0,1:T(8,128)} fusion(bf16[2,96,8192]{2,1,0:T(8,128)(2,1)S(1)} %copy-done, f32[2,96,512]{2,1,0:T(8,128)S(1)} %get-tuple-element.15, f32[1,96,512]{2,1,0:T(8,128)} %fusion.9, f32[1,96,512]{2,1,0:T(8,128)} %copy-done.1, f32[2,512]{1,0:T(2,128)S(1)} %broadcast_multiply_fusion, ...), kind=kOutput, calls=%fused_computation | convolution fusion | flops 1611399168 | bytes 20725760 | tf_op jit(solution)/shard_map/vrk,vrc->kc/dot_general | solution.py:67
  388.3 77.8 %psum.39 = f32[]{:T(128)} all-reduce(f32[]{:T(128)} %get-tuple-element.10), channel_id=1, replica_groups=mesh['dp'=16,'mp'=16] {'dp','mp'}, use_global_device_ids=true, to_apply=%region_11.12 | all-reduce | flops 1 | bytes 8 | tf_op jit(solution)/shard_map/psum | solution.py:42
  466.8 35.6 %reduce-scatter.5.cloned.1.call-done = f32[512,512]{0,1:T(8,128)} async-done(((f32[8192,512]{0,1:T(8,128)}), f32[512,512]{0,1:T(8,128)}) %reduce-scatter.5.cloned.1.call-update) | async-done | bytes 1048592 | tf_op jit(solution)/shard_map/reduce_scatter | solution.py:66
  502.3 2.5 copy.6
  (21 shorter events, 2.4 us)
Async XLA Ops:
  7.2 1.9 copy-start
  7.2 123.3 %all-gather.8.cloned.1.call-start = ((), (), s32[]{:S(2)}) async-start(), calls=%async_computation.6 | async-start | bytes 1671168 | tf_op jit(solution)/shard_map/all_gather | solution.py:25
  91.0 0.7 copy-start.2
  92.4 96.4 %all-gather.10.cloned.1.call-start = ((), (), s32[]{:S(2)}) async-start(), calls=%async_computation.7 | async-start | bytes 1671168 | tf_op jit(solution)/shard_map/all_gather | solution.py:27
  134.5 54.3 %all-to-all-start = ((bf16[96,16,512]{2,0,1:T(8,128)(2,1)}), bf16[96,16,512]{2,0,1:T(8,128)(2,1)}, u32[]{:S(2)}, u32[]{:S(2)}) async-start(bf16[96,16,512]{2,0,1:T(8,128)(2,1)} %copy.5), calls=%async_computation | async-start | bytes 3145728 | tf_op jit(solution)/shard_map/all_to_all | solution.py:26
  141.8 127.3 %all-gather.6.cloned.1.call-start = ((), (), s32[]{:S(2)}) async-start(), calls=%async_computation.3 | async-start | bytes 8912896 | tf_op jit(solution)/shard_map/all_gather | solution.py:47
  193.4 144.5 %reduce-scatter.3.cloned.1.call-start = ((), (), s32[]{:S(2)}) async-start(), calls=%async_computation.4 | async-start | bytes 3342336 | tf_op jit(solution)/shard_map/reduce_scatter | solution.py:52
  277.0 225.4 %reduce-scatter.5.cloned.1.call-start = ((), (), s32[]{:S(2)}) async-start(), calls=%async_computation.5 | async-start | bytes 17825792 | tf_op jit(solution)/shard_map/reduce_scatter | solution.py:66
  338.8 0.7 copy-start.1
Sparse Core Ops, SparseCore 0:
  92.5 37.9 all-gather.7
  133.5 55.2 all-gather.9
  193.5 75.5 all-gather.5
  277.1 60.7 reduce-scatter.2
  388.4 113.8 reduce-scatter.4
where the time goes:
time: 514 us; the launch traced here: 513 us
  waiting for transfers between devices  251 us (49%)
  blocking collectives  192 us (37%)
  matrix products  32.7 us (6%)
  between operations  15.6 us (3%)
  local copies, waits for them, and re-layouts  10.4 us (2%)
  starting transfers between devices  7.47 us (1%)
    psum x1, blocking collectives, body(): loss_value = lax.psum(jnp.sum(terms), ('dp', 'mp')) / full_width  77.8 us
    all_gather x1, waiting for transfers between devices, body(): incoming = lax.all_gather(corr_grad, 'dp', axis=0, tiled=True)  75.7 us
    reduce_scatter x1, waiting for transfers between devices, body(): lax.psum_scatter(across, 'mp', scatter_dimension=1, tiled=True) / batch_size  54.8 us
    all_gather x1, waiting for transfers between devices, body(): second_cols = lax.all_gather(normed[1], 'dp', axis=0, tiled=True)  47 us
    psum x1, blocking collectives, body(): spread = lax.psum(jnp.sum(shifted * shifted, axis=1), 'dp')  38.9 us
    psum x1, blocking collectives, body(): sum_first = lax.psum(jnp.sum(projected, axis=1), 'dp')  37.7 us
    all_gather x1, waiting for transfers between devices, body(): first_full = lax.all_gather(normed[0], 'mp', axis=1, tiled=True)  37.3 us
    psum x1, blocking collectives, body(): lax.psum((jnp.sum(normed_grad, axis=1), jnp.sum(normed_grad * centered, a...  37.3 us
  transfers between devices with their start and end apart: 6, of which 5 were waited for; matrix products, arithmetic and copies ran while one was open for 2% of the time, Pallas kernels for 0%

commit v1 on v0

v1 whole, which is shorter than its diff:
```python
import jax
import jax.numpy as jnp
from jax import lax
from jax.sharding import PartitionSpec as P

epsilon = 1e-05
off_weight = 0.0051


def body(features, weight):
    n_dp = lax.axis_size("dp")
    n_mp = lax.axis_size("mp")
    rows = features.shape[1]
    full_width = features.shape[2]
    cols = weight.shape[1]
    batch = rows * n_dp
    swap = [(a * n_mp + b, b * n_mp + a) for a in range(n_dp) for b in range(n_mp)]

    features_cols = lax.all_to_all(features, "dp", split_axis=2, concat_axis=1, tiled=True)
    projected = jnp.einsum("vrk,kc->vrc", features, weight, preferred_element_type=jnp.float32)
    local_mean = jnp.mean(projected, axis=1)
    local_dev = projected - local_mean[:, None, :]
    local_m2 = jnp.sum(local_dev * local_dev, axis=1)
    stats = lax.all_gather(jnp.stack([local_mean, local_m2]), "dp", axis=0)
    mean = jnp.mean(stats[:, 0], axis=0)
    gap = stats[:, 0] - mean[None]
    variance = (jnp.sum(stats[:, 1], axis=0) + rows * jnp.sum(gap * gap, axis=0)) / batch
    inv_std = lax.rsqrt(variance + epsilon)
    centered = (projected - mean[:, None, :]) * inv_std[:, None, :]
    normed = centered.astype(jnp.bfloat16)
    second_cols = lax.all_gather(normed[1], "dp", axis=0, tiled=True)
    first_block = lax.all_gather(
        lax.ppermute(normed[0], ("dp", "mp"), swap), "mp", axis=0, tiled=True
    )
    correlation = (
        lax.dot_general(
            first_block, second_cols, (((0,), (0,)), ((), ())), preferred_element_type=jnp.float32
        )
        / batch
    )
    row_ids = lax.axis_index("dp") * cols + lax.broadcasted_iota(jnp.int32, (cols, cols), 0)
    col_ids = lax.axis_index("mp") * cols + lax.broadcasted_iota(jnp.int32, (cols, cols), 1)
    on_diagonal = row_ids == col_ids
    terms = jnp.where(on_diagonal, (1.0 - correlation) ** 2, off_weight * correlation * correlation)
    loss_value = lax.psum(jnp.sum(terms), ("dp", "mp")) / full_width
    corr_grad = jnp.where(
        on_diagonal, 2.0 * (correlation - 1.0), 2.0 * off_weight * correlation
    ).astype(jnp.bfloat16)
    wide_grad = corr_grad.astype(jnp.float32)
    first_sum = jnp.sum(first_block.astype(jnp.float32), axis=0)
    second_sum = jnp.sum(second_cols.astype(jnp.float32), axis=0)
    across_second = lax.psum(
        jnp.stack(
            [jnp.sum(wide_grad * first_sum[:, None], axis=0) / batch, jnp.sum(wide_grad * correlation, axis=0)]
        ),
        "dp",
    )
    across_first = lax.psum(
        jnp.stack(
            [jnp.sum(wide_grad * second_sum[None, :], axis=1) / batch, jnp.sum(wide_grad * correlation, axis=1)]
        ),
        "mp",
    )
    part_second = jnp.dot(first_block, corr_grad, preferred_element_type=jnp.float32)
    part_first = lax.dot_general(
        second_cols, corr_grad, (((1,), (1,)), ((), ())), preferred_element_type=jnp.float32
    )
    grad_second = lax.psum_scatter(part_second, "dp", scatter_dimension=0, tiled=True) / batch
    grad_first = lax.psum_scatter(part_first, "mp", scatter_dimension=0, tiled=True) / batch
    grad_first, across_first = lax.ppermute((grad_first, across_first), ("dp", "mp"), swap)
    normed_grad = jnp.stack([grad_first, grad_second])
    across = jnp.stack([across_first, across_second])
    out_grad = (
        inv_std[:, None, :]
        * (
            normed_grad
            - across[:, 0][:, None, :] / batch
            - centered * (across[:, 1][:, None, :] / batch)
        )
    ).astype(jnp.bfloat16)
    out_cols = lax.all_gather(out_grad, "dp", axis=1, tiled=True)
    grad_weight = jnp.einsum("vrk,vrc->kc", features_cols, out_cols, preferred_element_type=jnp.float32)
    return (grad_weight, loss_value)


def solution(mesh):
    placed = (P(None, "dp", None), P(None, "mp"))
    return jax.shard_map(
        body, mesh=mesh, in_specs=placed, out_specs=(P("dp", "mp"), P()), check_vma=False
    )
```

time: 514 us -> 467 us (0.909)
  waiting for transfers between devices: 251 us -> 169 us
  blocking collectives: 192 us -> 224 us
  local copies, waits for them, and re-layouts: 10.4 us -> 24.1 us
  matrix products: 32.7 us -> 19.9 us
    all_gather x2, waiting for transfers between devices: 113 us -> 39 us  [the longest x1 39 us: body(): lax.all_gather(lax.ppermute(normed[0], ('dp', 'mp'), swap), 'mp', axis=0,...]
    all_to_all x0 -> x1, blocking collectives: none -> 64.6 us  [body(): lax.all_to_all(features, 'dp', split_axis=2, concat_axis=1, tiled=True)]
    psum x3 -> x2, blocking collectives: 114 us -> 61.2 us  [the longest x1 36.4 us: body(): lax.psum(jnp.stack([jnp.sum(wide_grad * first_sum[:, None], axis=0) / bat...]
    all_gather x0 -> x1, blocking collectives: none -> 23.7 us  [body(): stats = lax.all_gather(jnp.stack([local_mean, local_m2]), 'dp', axis=0)]
    dot_general x3, matrix products: 23 us -> 10.1 us  [the longest x1 4.69 us: body(): jnp.einsum('vrk,vrc->kc', features_cols, out_cols, preferred_element_type...]
    reduce_scatter x2, waiting for transfers between devices: 90.4 us -> 83 us  [the longest x1 82.9 us: body(): lax.psum_scatter(part_second, 'dp', scatter_dimension=0, tiled=True) / batch]
    all_to_all x1 -> x0, starting transfers between devices: 7.27 us -> none  [body(): lax.all_to_all(first_full, 'dp', split_axis=1, concat_axis=0, tiled=True)]
    all_to_all x1, local copies, waits for them, and re-layouts: 2 us -> 9.15 us  [body(): lax.all_to_all(features, 'dp', split_axis=2, concat_axis=1, tiled=True)]
  transfers between devices with their start and end apart: 6 -> 8, of which waited for: 5 -> 4; matrix products, arithmetic and copies ran while one was open for 2% -> 5% of each run, Pallas kernels for 0% -> 0%
where the time goes in v1:
time: 467 us; the launch traced here: 465 us
  blocking collectives  224 us (48%)
  waiting for transfers between devices  169 us (36%)
  local copies, waits for them, and re-layouts  24.1 us (5%)
  matrix products  19.9 us (4%)
  between operations  15.7 us (3%)
  other arithmetic  6.44 us (1%)
  starting transfers between devices  5.96 us (1%)
    reduce_scatter x1, waiting for transfers between devices, body(): lax.psum_scatter(part_second, 'dp', scatter_dimension=0, tiled=True) / batch  82.9 us
    psum x1, blocking collectives, body(): loss_value = lax.psum(jnp.sum(terms), ('dp', 'mp')) / full_width  74.4 us
    all_to_all x1, blocking collectives, body(): lax.all_to_all(features, 'dp', split_axis=2, concat_axis=1, tiled=True)  64.6 us
    all_gather x1, waiting for transfers between devices, body(): second_cols = lax.all_gather(normed[1], 'dp', axis=0, tiled=True)  43.2 us
    all_gather x1, waiting for transfers between devices, body(): lax.all_gather(lax.ppermute(normed[0], ('dp', 'mp'), swap), 'mp', axis=0,...  39 us
    psum x1, blocking collectives, body(): lax.psum(jnp.stack([jnp.sum(wide_grad * first_sum[:, None], axis=0) / bat...  36.4 us
    psum x1, blocking collectives, body(): lax.psum(jnp.stack([jnp.sum(wide_grad * second_sum[None, :], axis=1) / ba...  24.8 us
    all_gather x1, blocking collectives, body(): stats = lax.all_gather(jnp.stack([local_mean, local_m2]), 'dp', axis=0)  23.7 us
  transfers between devices with their start and end apart: 8, of which 4 were waited for; matrix products, arithmetic and copies ran while one was open for 5% of the time, Pallas kernels for 0%

profile of v1, /device:TPU:2, one launch (start us, length us, event | category | flops | bytes accessed | tf_op | source)
XLA Modules:
  0.0 465.1 jit_solution(12397336596627400424)
XLA Ops:
  7.2 6.1 %fusion.27 = (f32[2,512]{1,0:T(2,128)S(1)}, f32[2,96,512]{2,1,0:T(8,128)S(1)}) fusion(bf16[2,96,8192]{2,1,0:T(8,128)(2,1)} %param.2, bf16[8192,512]{1,0:T(8,128)(2,1)} %param.3), kind=kOutput, calls=%fused_computation.57 | convolution fusion | flops 1610710016 | bytes 11931648 | tf_op jit(solution)/shard_map/vrk,kc->vrc/dot_general | solution.py:20
  13.4 23.7 %all-gather = f32[32,2,512]{2,1,0:T(2,128)S(1)} all-gather(f32[2,2,512]{2,1,0:T(2,128)S(1)} %pad_maximum_fusion), channel_id=2, replica_groups=mesh['dp'=16,'mp'=16] {'dp'}, dimensions={0}, use_global_device_ids=true | all-gather | bytes 139264 | tf_op jit(solution)/shard_map/all_gather | solution.py:24
  38.0 1.9 collective-permute-start
  39.9 4.0 collective-permute-done
  44.7 43.2 %all-gather.10.cloned.1.call-done = bf16[1,1536,512]{2,1,0:T(8,128)(2,1)} async-done(((bf16[1,96,512]{2,1,0:T(8,128)(2,1)}), bf16[1,1536,512]{2,1,0:T(8,128)(2,1)}) %all-gather.10.cloned.1.call-update) | async-done | bytes 1572880 | tf_op jit(solution)/shard_map/all_gather | solution.py:31
  87.8 1.8 convert_reduce_fusion.1
  89.6 39.0 %all-gather.6.cloned.1.call-done = bf16[1536,512]{1,0:T(8,128)(2,1)} async-done(((bf16[96,512]{1,0:T(8,128)(2,1)}), bf16[1536,512]{1,0:T(8,128)(2,1)}) %all-gather.6.cloned.1.call-update) | async-done | bytes 1572880 | tf_op jit(solution)/shard_map/all_gather | solution.py:32
  128.6 1.7 convert_reduce_fusion
  130.3 3.7 fusion.12
  134.0 2.7 fusion.2
  136.7 1.3 copy-done.1
  138.1 2.7 fusion.28
  140.9 24.8 %psum.21 = f32[2,512]{1,0:T(2,128)S(1)} all-reduce(f32[2,512]{1,0:T(2,128)S(1)} %pad_maximum_fusion.2), channel_id=1, replica_groups=mesh['dp'=16,'mp'=16] {'mp'}, use_global_device_ids=true, to_apply=%region_10.11 | all-reduce | flops 1024 | bytes 8192 | tf_op jit(solution)/shard_map/psum | solution.py:58
  165.7 1.9 collective-permute-start.2
  167.6 36.4 %psum.22 = f32[1,2,512]{2,0,1:T(1,128)S(1)} all-reduce(f32[1,2,512]{2,0,1:T(1,128)S(1)} %stack.49), channel_id=1, replica_groups=mesh['dp'=16,'mp'=16] {'dp'}, use_global_device_ids=true, to_apply=%region_14.15 | all-reduce | flops 1024 | bytes 8192 | tf_op jit(solution)/shard_map/psum | solution.py:52
  204.1 0.9 broadcast_multiply_fusion
  205.0 1.9 collective-permute-start.1
  207.0 82.9 %reduce-scatter.5.cloned.1.call-done = f32[96,512]{1,0:T(8,128)} async-done(((f32[1536,512]{1,0:T(8,128)}), f32[96,512]{1,0:T(8,128)}) %reduce-scatter.5.cloned.1.call-update) | async-done | bytes 196624 | tf_op jit(solution)/shard_map/reduce_scatter | solution.py:68
  291.7 9.7 %copy.6 = bf16[2,96,8192]{1,0,2:T(2,128)(2,1)} copy(bf16[2,96,8192]{2,1,0:T(8,128)(2,1)} %param.2) | data formatting | bytes 6291456 | tf_op args[0]
  301.4 64.6 %all_to_all.18 = bf16[2,96,8192]{1,0,2:T(2,128)(2,1)} all-to-all(bf16[2,96,8192]{1,0,2:T(2,128)(2,1)} %copy.6), channel_id=1, replica_groups=mesh['dp'=16,'mp'=16] {'dp'}, dimensions={2} | all-to-all | bytes 6291456 | tf_op jit(solution)/shard_map/all_to_all | solution.py:19
  366.0 9.2 %copy.7 = bf16[2,96,16,512]{3,1,2,0:T(8,128)(2,1)S(1)} copy(bf16[2,96,16,512]{1,0,3,2:T(2,128)(2,1)} %bitcast.51) | data formatting | bytes 6291456 | tf_op jit(solution)/shard_map/all_to_all | solution.py:19
  375.2 74.4 %psum.23 = f32[]{:T(128)} all-reduce(f32[]{:T(128)} %get-tuple-element.8), channel_id=1, replica_groups=mesh['dp'=16,'mp'=16] {'dp','mp'}, use_global_device_ids=true, to_apply=%region_16.17 | all-reduce | flops 1 | bytes 8 | tf_op jit(solution)/shard_map/psum | solution.py:45
  450.2 4.7 %convolution_bitcast_fusion = f32[512,512]{0,1:T(8,128)} fusion(bf16[2,1536,512]{2,1,0:T(8,128)(2,1)} %all-gather.8.cloned.1.call-done, bf16[2,1536,512]{2,1,0:T(8,128)(2,1)S(1)} %bitcast.52), kind=kOutput, calls=%fused_computation.11 | convolution fusion | flops 1610612736 | bytes 7340032 | tf_op jit(solution)/shard_map/vrk,vrc->kc/dot_general | solution.py:82
  454.9 2.5 copy.8
  (38 shorter events, 3.6 us)
Async XLA Ops:
  7.2 80.7 %all-gather.10.cloned.1.call-start = ((), (), s32[]{:S(2)}) async-start(), calls=%async_computation.7 | async-start | bytes 1671168 | tf_op jit(solution)/shard_map/all_gather | solution.py:31
  38.0 90.7 %all-gather.6.cloned.1.call-start = ((), (), s32[]{:S(2)}) async-start(), calls=%async_computation.3 | async-start | bytes 1671168 | tf_op jit(solution)/shard_map/all_gather | solution.py:32
  38.0 5.9 %collective-permute-start = (bf16[96,512]{1,0:T(8,128)(2,1)S(1)}, bf16[96,512]{1,0:T(8,128)(2,1)S(1)}, u32[]{:S(2)}, u32[]{:S(2)}) collective-permute-start(bf16[96,512]{1,0:T(8,128)(2,1)S(1)} %get-tuple-element.15), channel_id=1, source_target_pairs={{0,0},{1,16},{2,32},{3,48},{4,64},{5,80},{6,96},{7,112},{8,128},{9... | collective-permute-start | bytes 294920 | tf_op jit(solution)/shard_map/ppermute | solution.py:33
  43.9 0.6 copy-start.2
  44.6 159.5 %reduce-scatter.3.cloned.1.call-start = ((), (), s32[]{:S(2)}) async-start(), calls=%async_computation.4 | async-start | bytes 3342336 | tf_op jit(solution)/shard_map/reduce_scatter | solution.py:69
  87.8 42.5 %copy-start = (bf16[1,1536,512]{2,1,0:T(8,128)(2,1)S(1)}, bf16[1,1536,512]{2,1,0:T(8,128)(2,1)}, u32[]{:S(2)}) copy-start(bf16[1,1536,512]{2,1,0:T(8,128)(2,1)} %all-gather.10.cloned.1.call-done) | copy-start | bytes 4718596
  136.7 1.4 copy-start.1
  136.7 153.2 %reduce-scatter.5.cloned.1.call-start = ((), (), s32[]{:S(2)}) async-start(), calls=%async_computation.5 | async-start | bytes 3342336 | tf_op jit(solution)/shard_map/reduce_scatter | solution.py:68
  140.8 309.5 %all-gather.8.cloned.1.call-start = ((), (), s32[]{:S(2)}) async-start(), calls=%async_computation.6 | async-start | bytes 3342336 | tf_op jit(solution)/shard_map/all_gather | solution.py:81
  165.7 38.3 %collective-permute-start.2 = (f32[2,512]{1,0:T(2,128)S(1)}, f32[2,512]{1,0:T(2,128)S(1)}, u32[]{:S(2)}, u32[]{:S(2)}) collective-permute-start(f32[2,512]{1,0:T(2,128)S(1)} %psum.21), channel_id=1, source_target_pairs={{0,0},{1,16},{2,32},{3,48},{4,64},{5,80},{6,96},{7,112},{8,128},{9... | collective-permute-start | bytes 12296 | tf_op jit(solution)/shard_map/ppermute | solution.py:70
  205.0 85.8 %collective-permute-start.1 = (f32[96,512]{1,0:T(8,128)S(1)}, f32[96,512]{1,0:T(8,128)S(1)}, u32[]{:S(2)}, u32[]{:S(2)}) collective-permute-start(f32[96,512]{1,0:T(8,128)S(1)} %broadcast_multiply_fusion), channel_id=1, source_target_pairs={{0,0},{1,16},{2,32},{3,48},{4,64},{5,80},{6,96},{7,112},{8,128},{9... | collective-permute-start | bytes 589832 | tf_op jit(solution)/shard_map/ppermute | solution.py:70
Sparse Core Ops, SparseCore 0:
  38.1 49.7 all-gather.9
  89.7 38.9 all-gather.5
  136.8 59.6 reduce-scatter.2
  200.0 89.8 reduce-scatter.4
  292.8 76.7 all-gather.7

commit v2 on v0

v2 whole, which is shorter than its diff:
```python
import functools

import jax
import jax.numpy as jnp
from jax import lax
from jax.experimental import pallas as pl
from jax.experimental.pallas import tpu as pltpu
from jax.sharding import PartitionSpec as P

epsilon = 1e-05
off_weight = 0.0051
SIDE = 4
CORES = 2
STAT = 8
MSGS = 160
MESH = pl.DeviceIdType.MESH


class Mail:
    def __init__(self, send_sem, recv_sem):
        self.send_sem, self.recv_sem, self.sent = send_sem, recv_sem, []

    def push(self, src, dst, device):
        index = len(self.sent)
        copy = pltpu.make_async_remote_copy(
            src_ref=src,
            dst_ref=dst,
            send_sem=self.send_sem.at[index],
            recv_sem=self.recv_sem.at[index],
            device_id=device,
            device_id_type=MESH,
        )
        copy.start()
        self.sent.append(copy)
        return copy

    def close(self):
        for copy in self.sent:
            copy.wait_send()


def kernel(
    n_dp,
    n_mp,
    features,
    weight,
    grad,
    loss,
    w_buf,
    f_buf,
    cent,
    stat_x,
    stat_y,
    inv_buf,
    turn_out,
    t0,
    t1,
    corr_buf,
    g_buf,
    p0,
    p1_buf,
    opp_l,
    opp_r,
    fin_l,
    fin_r,
    opp2_l,
    opp2_r,
    fin2_l,
    fin2_r,
    sib,
    up_a,
    up_b,
    down_a,
    down_b,
    turn_back,
    og,
    fk,
    loss_x,
    loss_y,
    loss_z,
    loss_c,
    send_sem,
    recv_sem,
    load_sem,
    turn_sem,
):
    rows = cent.shape[1]
    cols = cent.shape[2]
    depth = features.shape[2]
    batch = rows * n_dp
    ring = n_mp // CORES
    piece = rows + STAT
    top = piece // 2 // 8 * 8 + (8 if piece // 2 % 8 else 0)

    i = lax.axis_index("dp")
    j = lax.axis_index("mp")
    y, x = i // SIDE, i % SIDE
    z, c = j // CORES, j % CORES
    q1 = x * (1 - c) + y * c
    q2 = y * (1 - c) + x * c
    s1 = 1 * (1 - c) + SIDE * c
    s2 = SIDE * (1 - c) + 1 * c

    def ring1(q):
        return (q * s1 + q2 * s2, j)

    def ring2(q):
        return (q1 * s1 + q * s2, j)

    def zdev(q):
        return (i, q * CORES + c)

    def slot_of(a, core):
        ay, ax = a // SIDE, a % SIDE
        return (ax * SIDE + ay) * (1 - core) + a * core

    right1, left1, far1 = (q1 + 1) % SIDE, (q1 + SIDE - 1) % SIDE, (q1 + 2) % SIDE
    right2, left2, far2 = (q2 + 1) % SIDE, (q2 + SIDE - 1) % SIDE, (q2 + 2) % SIDE
    up, down = (z + 1) % ring, (z + ring - 1) % ring
    sibling = (i, z * CORES + 1 - c)
    mail = Mail(send_sem, recv_sem)

    barrier = pltpu.get_barrier_semaphore()
    for d in range(1, n_dp):
        pl.semaphore_signal(barrier, inc=1, device_id=((i + d) % n_dp, j), device_id_type=MESH)
    for d in range(1, ring):
        pl.semaphore_signal(barrier, inc=1, device_id=zdev((z + d) % ring), device_id_type=MESH)
    pl.semaphore_signal(barrier, inc=1, device_id=sibling, device_id_type=MESH)

    @pl.when(i != j)
    def _():
        pl.semaphore_signal(barrier, inc=1, device_id=(j, i), device_id_type=MESH)

    parts = 8
    step = depth // parts

    def loads(k):
        cut = pl.ds(pl.multiple_of(k * step, step), step)
        return (
            pltpu.make_async_copy(weight.at[cut, :], w_buf.at[cut, :], load_sem.at[k]),
            pltpu.make_async_copy(
                features.at[:, :, cut], f_buf.at[:, :, cut], load_sem.at[parts + k]
            ),
        )

    for k in range(parts):
        for load in loads(k):
            load.start()
    own_k = pltpu.make_async_copy(
        features.at[c, :, pl.ds(pl.multiple_of(i * cols, cols), cols)],
        fk.at[c, i],
        load_sem.at[2 * parts],
    )
    own_k.start()

    greeted = n_dp - 1 + ring - 1 + 1

    @pl.when(i != j)
    def _():
        pl.semaphore_wait(barrier, greeted + 1)

    @pl.when(i == j)
    def _():
        pl.semaphore_wait(barrier, greeted)

    cent[...] = jnp.zeros_like(cent)

    def project(k, carry):
        for load in loads(k):
            load.wait()
        cut = pl.ds(pl.multiple_of(k * step, step), step)
        left = f_buf[:, :, cut].reshape(2 * rows, step)
        got = jnp.dot(left, w_buf[cut, :], preferred_element_type=jnp.float32)
        cent[...] += got.reshape(2, rows, cols)
        return carry

    lax.fori_loop(0, parts, project, 0)

    projected = cent[...]
    mean = jnp.sum(projected, axis=1) / rows
    shifted = projected - mean[:, None, :]
    spread = jnp.sum(shifted * shifted, axis=1)
    pad = jnp.zeros((STAT - 4, cols), jnp.float32)
    for buf, at, stride, count in (
        (stat_x, x, 1, rows),
        (stat_y, y, SIDE, rows * SIDE),
    ):
        buf[at] = jnp.concatenate([mean, spread, pad], axis=0)
        copies = []
        for d in range(1, SIDE):
            other = (at + d) % SIDE
            copies.append(mail.push(buf.at[at], buf.at[at], (i + (other - at) * stride, j)))
        for copy in copies:
            copy.wait_recv()
        got = buf[...]
        mean = (got[0, 0:2] + got[1, 0:2] + got[2, 0:2] + got[3, 0:2]) / SIDE
        spread = got[0, 2:4] + got[1, 2:4] + got[2, 2:4] + got[3, 2:4]
        for s in range(SIDE):
            gap = got[s, 0:2] - mean
            spread = spread + count * (gap * gap)
    inv_std = lax.rsqrt(spread / batch + epsilon)
    inv_buf[0:2] = inv_std
    centered = (projected - mean[:, None, :]) * inv_std[:, None, :]
    cent[...] = centered
    normed = centered.astype(jnp.bfloat16)
    own = q1 * SIDE + q2
    turn_out[...] = normed[0]
    t1[own] = normed[1]

    turn_slot = slot_of(j, c)
    partner_slot = slot_of(i, i % CORES)
    go = pltpu.make_async_remote_copy(
        src_ref=turn_out,
        dst_ref=t0.at[partner_slot],
        send_sem=turn_sem.at[0],
        recv_sem=turn_sem.at[1],
        device_id=(j, i),
        device_id_type=MESH,
    )
    stay = pltpu.make_async_copy(turn_out, t0.at[turn_slot], turn_sem.at[2])

    @pl.when(i != j)
    def _():
        go.start()

    @pl.when(i == j)
    def _():
        stay.start()

    half = rows // 2

    def spread2(slot):
        return (
            mail.push(t1.at[slot], t1.at[slot], ring2(right2)),
            mail.push(t1.at[slot], t1.at[slot], ring2(left2)),
        )

    a1 = mail.push(t1.at[own], t1.at[own], ring1(right1))
    b1 = mail.push(t1.at[own], t1.at[own], ring1(left1))
    second = [spread2(own)]

    @pl.when(i != j)
    def _():
        go.wait_recv()

    @pl.when(i == j)
    def _():
        stay.wait()

    z_up = [mail.push(t0.at[turn_slot], t0.at[turn_slot], zdev(up))]
    z_down = [mail.push(t0.at[turn_slot], t0.at[turn_slot], zdev(down))]
    side_copies = []

    def to_side(q):
        a = q * CORES + c
        side_copies.append(
            mail.push(t0.at[slot_of(a, c)], t0.at[slot_of(a, 1 - c)], sibling)
        )

    to_side(z)

    a1.wait_recv()
    from_left = left1 * SIDE + q2
    c1 = mail.push(
        t1.at[from_left, pl.ds(0, half)], t1.at[from_left, pl.ds(0, half)], ring1(right1)
    )
    second.append(spread2(from_left))
    b1.wait_recv()
    from_right = right1 * SIDE + q2
    d1 = mail.push(
        t1.at[from_right, pl.ds(half, half)], t1.at[from_right, pl.ds(half, half)], ring1(left1)
    )
    second.append(spread2(from_right))

    far = ring // 2
    for t in range(1, far):
        low, high = (z + ring - t) % ring, (z + t) % ring
        low_slot, high_slot = slot_of(low * CORES + c, c), slot_of(high * CORES + c, c)
        z_up[-1].wait_recv()
        if t < far - 1:
            z_up.append(mail.push(t0.at[low_slot], t0.at[low_slot], zdev(up)))
        else:
            part = t0.at[low_slot, pl.ds(0, half)]
            z_up.append(mail.push(part, part, zdev(up)))
        z_down[-1].wait_recv()
        if t < far - 1:
            z_down.append(mail.push(t0.at[high_slot], t0.at[high_slot], zdev(down)))
        else:
            part = t0.at[high_slot, pl.ds(half, half)]
            z_down.append(mail.push(part, part, zdev(down)))
        to_side(low)
        to_side(high)
        if t == 1:
            c1.wait_recv()
            d1.wait_recv()
            second.append(spread2(far1 * SIDE + q2))

    forwards = []
    for n, (q, pair) in enumerate(zip((q1, left1, right1, far1), second)):
        to_right, to_left = pair
        to_right.wait_recv()
        if n in (0, 3):
            part = t1.at[q * SIDE + left2]
            forwards.append(mail.push(part, part, ring2(right2)))
        to_left.wait_recv()
        if n in (1, 2):
            part = t1.at[q * SIDE + right2]
            forwards.append(mail.push(part, part, ring2(left2)))

    own_k.wait()
    feature_copies = []
    for d in range(1, n_dp):
        other = (i + d) % n_dp
        feature_copies.append(
            mail.push(
                features.at[c, :, pl.ds(pl.multiple_of(other * cols, cols), cols)],
                fk.at[c, i],
                (other, j),
            )
        )

    z_up[-1].wait_recv()
    z_down[-1].wait_recv()
    to_side((z + far) % ring)
    for copy in forwards:
        copy.wait_recv()
    for copy in side_copies:
        copy.wait_recv()

    tile = 128
    tiles = cols // tile
    col_ids = j * cols + lax.broadcasted_iota(jnp.int32, (tile, cols), 1)

    def correlate(t, carry):
        total, cross_cols = carry
        cut = pl.ds(pl.multiple_of(t * tile, tile), tile)
        left = t0[:, :, cut].reshape(batch, tile)
        corr = lax.dot_general(
            left, t1[...].reshape(batch, cols), (((0,), (0,)), ((), ())),
            preferred_element_type=jnp.float32,
        ) * (1.0 / batch)
        row_ids = i * cols + t * tile + lax.broadcasted_iota(jnp.int32, (tile, cols), 0)
        on_diagonal = row_ids == col_ids
        gap = corr - 1.0
        terms = jnp.where(on_diagonal, gap * gap, off_weight * corr * corr)
        g = jnp.where(on_diagonal, 2.0 * gap, 2.0 * off_weight * corr).astype(jnp.bfloat16)
        g_buf[pl.ds(pl.multiple_of(t * tile, tile), tile), :] = g
        both = g.astype(jnp.float32) * corr
        corr_buf[pl.ds(pl.multiple_of(t * tile, tile), tile), :] = jnp.broadcast_to(
            jnp.sum(both, axis=1, keepdims=True), (tile, tile)
        )
        return (
            total + jnp.sum(terms, axis=0, keepdims=True),
            cross_cols + jnp.sum(both, axis=0, keepdims=True),
        )

    nothing = jnp.zeros((1, cols), jnp.float32)
    total, cross_cols = lax.fori_loop(0, tiles, correlate, (nothing, nothing))
    cross_rows = corr_buf[...].T[0:1, :]
    g_all = g_buf[...]

    def three(v):
        high = v.astype(jnp.bfloat16)
        rest = v - high.astype(jnp.float32)
        mid = rest.astype(jnp.bfloat16)
        low = (rest - mid.astype(jnp.float32)).astype(jnp.bfloat16)
        return jnp.concatenate([high, mid, low, jnp.zeros((13, cols), jnp.bfloat16)], axis=0)

    def add_rows(n, carry):
        first, other = carry
        return (
            first + jnp.sum(t0[n].astype(jnp.float32), axis=0, keepdims=True),
            other + jnp.sum(t1[n].astype(jnp.float32), axis=0, keepdims=True),
        )

    sum0, sum1 = lax.fori_loop(0, n_dp, add_rows, (nothing, nothing))
    down_g = jnp.dot(three(sum0), g_all, preferred_element_type=jnp.float32)
    across_g = lax.dot_general(
        three(sum1), g_all, (((1,), (1,)), ((), ())), preferred_element_type=jnp.float32
    )
    scale = 1.0 / batch
    blank = jnp.zeros((STAT - 2, cols), jnp.float32)
    stats1 = jnp.concatenate(
        [jnp.sum(down_g[0:3], axis=0, keepdims=True) * (scale * scale), cross_cols * scale, blank], axis=0
    )
    stats0 = jnp.concatenate(
        [jnp.sum(across_g[0:3], axis=0, keepdims=True) * (scale * scale), cross_rows * scale, blank], axis=0
    )

    def part1(q):
        cut = pl.ds(q * SIDE, SIDE)
        got = jnp.dot(
            t0[cut].reshape(SIDE * rows, cols), g_buf[...], preferred_element_type=jnp.float32
        )
        p1_buf[cut, 0:rows, :] = (got * scale).reshape(SIDE, rows, cols)
        p1_buf[cut, rows:piece, :] = jnp.broadcast_to(stats1[None], (SIDE, STAT, cols))

    def part0(q, carry):
        cut = pl.ds(q * SIDE, SIDE)
        got = lax.dot_general(
            t1[cut].reshape(SIDE * rows, cols), g_buf[...], (((1,), (1,)), ((), ())),
            preferred_element_type=jnp.float32,
        )
        p0[cut, 0:rows, :] = (got * scale).reshape(SIDE, rows, cols)
        p0[cut, rows:piece, :] = jnp.broadcast_to(stats0[None], (SIDE, STAT, cols))
        return carry

    part1(far1)
    far_r = [mail.push(p1_buf.at[far1 * SIDE + n], opp_l.at[n], ring1(right1)) for n in (0, 1)]
    far_l = [
        mail.push(p1_buf.at[far1 * SIDE + 2 + n], opp_r.at[n], ring1(left1)) for n in (0, 1)
    ]
    lax.fori_loop(0, SIDE, part0, 0)
    order = [(z + far) % ring]
    for t in range(far - 1, 0, -1):
        order += [(z + t) % ring, (z + ring - t) % ring]
    order.append(z)
    side = [
        mail.push(
            p0.at[slot_of(q * CORES + 1 - c, c)], sib.at[q], sibling
        )
        for q in order
    ]
    part1(right1)
    near_r = [None, None] + [
        mail.push(p1_buf.at[right1 * SIDE + n], fin_l.at[n], ring1(right1)) for n in (2, 3)
    ]
    part1(left1)
    near_l = [
        mail.push(p1_buf.at[left1 * SIDE + n], fin_r.at[n], ring1(left1)) for n in (0, 1)
    ] + [None, None]
    part1(q1)

    def loss_send(buf, at, others, value):
        buf[at] = value
        return [mail.push(buf.at[at], buf.at[at], device) for device in others]

    def loss_sum(buf, copies):
        for copy in copies:
            copy.wait_recv()
        value = buf[0]
        for n in range(1, buf.shape[0]):
            value = value + buf[n]
        return value

    mine = jnp.broadcast_to(jnp.sum(total, axis=1, keepdims=True), (8, 128))
    loss_copies = loss_send(
        loss_x, x, [(y * SIDE + (x + d) % SIDE, j) for d in range(1, SIDE)], mine
    )

    halves = (pl.ds(0, top), pl.ds(top, piece - top))

    def settle(n):
        side[n].wait_recv()
        q = order[n]
        at = slot_of(q * CORES + c, c)
        p0[at] = p0[at] + sib[q]

    settle(0)
    settle(1)
    settle(2)

    def row(q, h):
        return p0.at[slot_of(q * CORES + c, c), halves[h]]

    dest_up = lambda t: (z + t) % ring
    dest_down = lambda t: (z + ring - t) % ring
    chain_ua = [mail.push(row(dest_up(far), 0), up_a.at[0], zdev(up))]
    chain_db = [mail.push(row(dest_down(far), 1), down_b.at[0], zdev(down))]
    chain_ub = [mail.push(row(dest_up(far - 1), 1), up_b.at[0], zdev(up))]
    chain_da = [mail.push(row(dest_down(far - 1), 0), down_a.at[0], zdev(down))]
    for n in range(3, ring):
        settle(n)

    for n in (0, 1):
        far_r[n].wait_recv()
        at = right1 * SIDE + n
        p1_buf[at] = p1_buf[at] + opp_l[n]
        near_r[n] = mail.push(p1_buf.at[at], fin_l.at[n], ring1(right1))
        far_l[n].wait_recv()
        at = left1 * SIDE + 2 + n
        p1_buf[at] = p1_buf[at] + opp_r[n]
        near_l[2 + n] = mail.push(p1_buf.at[at], fin_r.at[2 + n], ring1(left1))

    def pass_on(chain, buf, h, dest, device):
        n = len(chain) - 1
        chain[n].wait_recv()
        at = slot_of(dest * CORES + c, c)
        p0[at, halves[h]] = p0[at, halves[h]] + buf[n]
        chain.append(mail.push(p0.at[at, halves[h]], buf.at[n + 1], device))

    total = loss_sum(loss_x, loss_copies)
    loss_copies = loss_send(
        loss_y, y, [(((y + d) % SIDE) * SIDE + x, j) for d in range(1, SIDE)], total
    )

    for t in range(far - 1, 0, -1):
        pass_on(chain_ua, up_a, 0, dest_up(t), zdev(up))
        pass_on(chain_db, down_b, 1, dest_down(t), zdev(down))
        if t > 1:
            pass_on(chain_ub, up_b, 1, dest_up(t - 1), zdev(up))
            pass_on(chain_da, down_a, 0, dest_down(t - 1), zdev(down))

    total = loss_sum(loss_y, loss_copies)
    loss_copies = loss_send(loss_z, z, [zdev((z + d) % ring) for d in range(1, ring)], total)

    for n in range(SIDE):
        near_r[n].wait_recv()
        near_l[n].wait_recv()
        at = q1 * SIDE + n
        p1_buf[at] = p1_buf[at] + fin_l[n] + fin_r[n]
    base = q1 * SIDE
    far2_r = mail.push(p1_buf.at[base + far2, halves[0]], opp2_l, ring2(right2))
    far2_l = mail.push(p1_buf.at[base + far2, halves[1]], opp2_r, ring2(left2))
    n2r = mail.push(
        p1_buf.at[base + right2, halves[1]], fin2_l.at[halves[1]], ring2(right2)
    )
    n2l = mail.push(p1_buf.at[base + left2, halves[0]], fin2_r.at[halves[0]], ring2(left2))
    far2_r.wait_recv()
    p1_buf[base + right2, halves[0]] = p1_buf[base + right2, halves[0]] + opp2_l[...]
    n2r2 = mail.push(
        p1_buf.at[base + right2, halves[0]], fin2_l.at[halves[0]], ring2(right2)
    )
    far2_l.wait_recv()
    p1_buf[base + left2, halves[1]] = p1_buf[base + left2, halves[1]] + opp2_r[...]
    n2l2 = mail.push(p1_buf.at[base + left2, halves[1]], fin2_r.at[halves[1]], ring2(left2))

    for chain in (chain_ua, chain_db, chain_ub, chain_da):
        chain[-1].wait_recv()
    mine_at = slot_of(j, c)
    p0[mine_at, halves[0]] = p0[mine_at, halves[0]] + up_a[far - 1] + down_a[far - 2]
    p0[mine_at, halves[1]] = p0[mine_at, halves[1]] + up_b[far - 2] + down_b[far - 1]
    back = pltpu.make_async_remote_copy(
        src_ref=p0.at[mine_at],
        dst_ref=turn_back,
        send_sem=turn_sem.at[3],
        recv_sem=turn_sem.at[4],
        device_id=(j, i),
        device_id_type=MESH,
    )
    back_stay = pltpu.make_async_copy(p0.at[mine_at], turn_back, turn_sem.at[5])

    @pl.when(i != j)
    def _():
        back.start()

    @pl.when(i == j)
    def _():
        back_stay.start()

    n2r.wait_recv()
    n2l.wait_recv()
    n2r2.wait_recv()
    n2l2.wait_recv()

    def finish(view, total):
        inv = inv_buf[view : view + 1]
        got = inv * (
            total[0:rows] - total[rows : rows + 1] - cent[view] * total[rows + 1 : rows + 2]
        )
        og[view, i] = got.astype(jnp.bfloat16)

    finish(1, p1_buf[base + q2] + fin2_l[...] + fin2_r[...])

    def index_of(a, b):
        return a * s1 + b * s2

    def gather_first(view):
        part = og.at[view, i]
        first = (mail.push(part, part, ring1(right1)), mail.push(part, part, ring1(left1)))
        return first

    def gather_second(view, a):
        part = og.at[view, index_of(a, q2)]
        return (mail.push(part, part, ring2(right2)), mail.push(part, part, ring2(left2)))

    def gather_mid(view, first):
        first[0].wait_recv()
        if view == 0:
            part = og.at[view, index_of(left1, q2)]
            last = mail.push(part, part, ring1(right1))
        sends = [gather_second(view, left1)]
        first[1].wait_recv()
        if view == 1:
            part = og.at[view, index_of(right1, q2)]
            last = mail.push(part, part, ring1(left1))
        sends.append(gather_second(view, right1))
        return last, sends

    def gather_pass(view, n, a, pair):
        pair[0].wait_recv()
        pair[1].wait_recv()
        if n % 2 == view:
            part = og.at[view, index_of(a, left2)]
            return mail.push(part, part, ring2(right2))
        part = og.at[view, index_of(a, right2)]
        return mail.push(part, part, ring2(left2))

    first1 = gather_first(1)
    own1 = gather_second(1, q1)
    last1, mid1 = gather_mid(1, first1)

    @pl.when(i != j)
    def _():
        back.wait_recv()

    @pl.when(i == j)
    def _():
        back_stay.wait()

    finish(0, turn_back[...])
    first0 = gather_first(0)
    own0 = gather_second(0, q1)

    total = loss_sum(loss_z, loss_copies)
    loss_copies = loss_send(loss_c, c, [sibling], total)

    last = []
    last.append(gather_pass(1, 0, q1, own1))
    last1.wait_recv()
    end1 = gather_second(1, far1)
    last0, mid0 = gather_mid(0, first0)
    last.append(gather_pass(1, 1, left1, mid1[0]))
    last.append(gather_pass(1, 2, right1, mid1[1]))
    last.append(gather_pass(0, 0, q1, own0))
    last0.wait_recv()
    end0 = gather_second(0, far1)

    for copy in feature_copies:
        copy.wait_recv()
    to_twin = mail.push(fk.at[c], fk.at[c], sibling)

    last.append(gather_pass(1, 3, far1, end1))
    last.append(gather_pass(0, 1, left1, mid0[0]))
    last.append(gather_pass(0, 2, right1, mid0[1]))
    last.append(gather_pass(0, 3, far1, end0))
    loss[...] = loss_sum(loss_c, loss_copies) / (n_mp * cols)
    for copy in last:
        copy.wait_recv()
    to_twin.wait_recv()

    def weigh(t, carry):
        cut = pl.ds(pl.multiple_of(t * tile, tile), tile)
        left = fk[:, :, :, cut].reshape(2 * batch, tile)
        grad[pl.ds(pl.multiple_of(t * tile, tile), tile), :] = lax.dot_general(
            left, og[...].reshape(2 * batch, cols), (((0,), (0,)), ((), ())),
            preferred_element_type=jnp.float32,
        )
        return carry

    lax.fori_loop(0, tiles, weigh, 0)

    @pl.when(i != j)
    def _():
        go.wait_send()
        back.wait_send()

    mail.close()


def body(n_dp, n_mp, features, weight):
    rows, depth = features.shape[1], features.shape[2]
    cols = weight.shape[1]
    ring = n_mp // CORES
    far = ring // 2
    piece = rows + STAT
    top = piece // 2 // 8 * 8 + (8 if piece // 2 % 8 else 0)
    f32, bf16 = jnp.float32, jnp.bfloat16
    V = pltpu.VMEM
    scratch = [
        V((depth, cols), bf16),
        V((2, rows, depth), bf16),
        V((2, rows, cols), f32),
        V((SIDE, STAT, cols), f32),
        V((SIDE, STAT, cols), f32),
        V((STAT, cols), f32),
        V((rows, cols), bf16),
        V((n_dp, rows, cols), bf16),
        V((n_dp, rows, cols), bf16),
        V((cols, 128), f32),
        V((cols, cols), bf16),
        V((n_dp, piece, cols), f32),
        V((n_dp, piece, cols), f32),
        V((2, piece, cols), f32),
        V((2, piece, cols), f32),
        V((SIDE, piece, cols), f32),
        V((SIDE, piece, cols), f32),
        V((top, cols), f32),
        V((piece - top, cols), f32),
        V((piece, cols), f32),
        V((piece, cols), f32),
        V((ring, piece, cols), f32),
        V((far, top, cols), f32),
        V((far - 1, piece - top, cols), f32),
        V((far - 1, top, cols), f32),
        V((far, piece - top, cols), f32),
        V((piece, cols), f32),
        V((2, n_dp, rows, cols), bf16),
        V((2, n_dp, rows, cols), bf16),
        V((SIDE, 8, 128), f32),
        V((SIDE, 8, 128), f32),
        V((ring, 8, 128), f32),
        V((CORES, 8, 128), f32),
        pltpu.SemaphoreType.DMA((MSGS,)),
        pltpu.SemaphoreType.DMA((MSGS,)),
        pltpu.SemaphoreType.DMA((17,)),
        pltpu.SemaphoreType.DMA((6,)),
    ]
    grad, loss = pl.pallas_call(
        functools.partial(kernel, n_dp, n_mp),
        out_shape=(
            jax.ShapeDtypeStruct((cols, cols), f32),
            jax.ShapeDtypeStruct((8, 128), f32),
        ),
        in_specs=[pl.BlockSpec(memory_space=pl.ANY)] * 2,
        out_specs=(pl.BlockSpec(memory_space=V), pl.BlockSpec(memory_space=V)),
        scratch_shapes=scratch,
        compiler_params=pltpu.CompilerParams(
            collective_id=0, has_side_effects=True, vmem_limit_bytes=60 * 2**20
        ),
    )(features, weight)
    return (grad, loss[0, 0])


def solution(mesh):
    placed = (P(None, "dp", None), P(None, "mp"))
    return jax.shard_map(
        functools.partial(body, mesh.shape["dp"], mesh.shape["mp"]),
        mesh=mesh,
        in_specs=placed,
        out_specs=(P("dp", "mp"), P()),
        check_vma=False,
    )
```

time: 514 us -> 150 us (0.29)
  waiting for transfers between devices: 251 us -> 0 us
  blocking collectives: 192 us -> 0 us
  Pallas kernels: 0 us -> 146 us
  matrix products: 32.7 us -> 0 us
  between operations: 15.6 us -> 0.64 us
  starting transfers between devices: 7.47 us -> 0 us
  local copies, waits for them, and re-layouts: 10.4 us -> 3.45 us
    psum x4 -> x0, blocking collectives: 192 us -> none  [the longest x1 77.8 us: body(): loss_value = lax.psum(jnp.sum(terms), ('dp', 'mp')) / full_width]
    all_gather x3 -> x0, waiting for transfers between devices: 160 us -> none  [the longest x1 75.7 us: body(): incoming = lax.all_gather(corr_grad, 'dp', axis=0, tiled=True)]
    pallas_call x0 -> x1, Pallas kernels: none -> 146 us  [body(): pl.pallas_call(functools.partial(kernel, n_dp, n_mp), out_shape=(jax.Shap...]
    reduce_scatter x2 -> x0, waiting for transfers between devices: 90.4 us -> none  [the longest x1 54.8 us: body(): lax.psum_scatter(across, 'mp', scatter_dimension=1, tiled=True) / batch_size]
    dot_general x5 -> x0, matrix products: 32.7 us -> none  [the longest x1 9.14 us: body(): jnp.einsum('vrk,vrc->kc', features, out_grad, preferred_element_type=jnp....]
    all_to_all x1 -> x0, starting transfers between devices: 7.27 us -> none  [body(): lax.all_to_all(first_full, 'dp', split_axis=1, concat_axis=0, tiled=True)]
    unnamed x8 -> x1, local copies, waits for them, and re-layouts: 7.7 us -> 2.26 us
  transfers between devices with their start and end apart: 6 -> 0, of which waited for: 5 -> 0; matrix products, arithmetic and copies ran while one was open for 2% -> 0% of each run, Pallas kernels for 0% -> 0%
where the time goes in v2:
time: 150 us
  Pallas kernels  146 us (97%)
  local copies, waits for them, and re-layouts  3.45 us (2%)
    pallas_call x1, Pallas kernels, body(): pl.pallas_call(functools.partial(kernel, n_dp, n_mp), out_shape=(jax.Shap...  146 us

profile of v2, /device:TPU:2, one launch (start us, length us, event | category | flops | bytes accessed | tf_op | source)
XLA Modules:
  0.0 150.3 jit_solution(3963817914878394290)
XLA Ops:
  0.6 146.3 %shard_map.41 = (f32[512,512]{1,0:T(8,128)}, f32[8,128]{1,0:T(8,128)}) custom-call(bf16[2,96,8192]{2,1,0:T(8,128)(2,1)} %features.1, bf16[8192,512]{1,0:T(8,128)(2,1)} %weight.1), custom_call_target="tpu_custom_call" | custom-call | tf_op jit(solution)/shard_map/pallas_call | solution.py:709
  146.9 1.2 slice.3
  148.1 2.3 %copy.5 = f32[512,512]{1,0:T(8,128)} copy(f32[512,512]{1,0:T(8,128)} %get-tuple-element.8) | data formatting | bytes 2097152

commit v3 on v0

v3 whole, which is shorter than its diff:
```python
import functools

import jax
import jax.numpy as jnp
from jax import lax
from jax.experimental import pallas as pl
from jax.experimental.pallas import tpu as pltpu
from jax.sharding import PartitionSpec as P

epsilon = 1e-05
off_weight = 0.0051
SIDE = 4
CORES = 2
LANES = 128
MSGS = 160
MESH = pl.DeviceIdType.MESH


class Mail:
    def __init__(self, send_sem, recv_sem):
        self.send_sem, self.recv_sem, self.sent = send_sem, recv_sem, []

    def push(self, src, dst, device):
        index = len(self.sent)
        copy = pltpu.make_async_remote_copy(
            src_ref=src,
            dst_ref=dst,
            send_sem=self.send_sem.at[index],
            recv_sem=self.recv_sem.at[index],
            device_id=device,
            device_id_type=MESH,
        )
        copy.start()
        self.sent.append(copy)
        return copy

    def close(self):
        for copy in self.sent:
            copy.wait_send()


def kernel(
    n_dp,
    n_mp,
    features,
    weight,
    grad,
    loss,
    w_buf,
    f_buf,
    acc,
    turned,
    arrived,
    cent,
    t0,
    t1,
    g_buf,
    gt_buf,
    p0,
    p1,
    opp_l,
    opp_r,
    fin_l,
    fin_r,
    opp2_l,
    opp2_r,
    fin2_l,
    fin2_r,
    sib,
    up_a,
    up_b,
    down_a,
    down_b,
    og,
    fk,
    loss_x,
    loss_y,
    loss_z,
    loss_c,
    send_sem,
    recv_sem,
    load_sem,
):
    rows = f_buf.shape[1]
    depth, cols = w_buf.shape
    batch = rows * n_dp
    sub = cols // n_dp
    ring = n_mp // CORES
    far = ring // 2
    scale = 1.0 / batch

    i = lax.axis_index("dp")
    j = lax.axis_index("mp")
    y, x = i // SIDE, i % SIDE
    z, c = j // CORES, j % CORES
    q1 = x * (1 - c) + y * c
    q2 = y * (1 - c) + x * c
    s1 = 1 * (1 - c) + SIDE * c
    s2 = SIDE * (1 - c) + 1 * c

    def index_of(a, b):
        return a * s1 + b * s2

    def ring1(q):
        return (index_of(q, q2), j)

    def ring2(q):
        return (index_of(q1, q), j)

    def zdev(q):
        return (i, q * CORES + c)

    right1, left1, far1 = (q1 + 1) % SIDE, (q1 + SIDE - 1) % SIDE, (q1 + 2) % SIDE
    right2, left2, far2 = (q2 + 1) % SIDE, (q2 + SIDE - 1) % SIDE, (q2 + 2) % SIDE
    up, down = (z + 1) % ring, (z + ring - 1) % ring
    sibling = (i, z * CORES + 1 - c)
    mail = Mail(send_sem, recv_sem)
    low, high = pl.ds(0, sub // 2), pl.ds(sub // 2, sub // 2)

    barrier = pltpu.get_barrier_semaphore()
    for d in range(1, n_dp):
        pl.semaphore_signal(barrier, inc=1, device_id=((i + d) % n_dp, j), device_id_type=MESH)
    for d in range(1, ring):
        pl.semaphore_signal(barrier, inc=1, device_id=zdev((z + d) % ring), device_id_type=MESH)
    pl.semaphore_signal(barrier, inc=1, device_id=sibling, device_id_type=MESH)

    parts = 8
    step = depth // parts

    def loads(k):
        cut = pl.ds(pl.multiple_of(k * step, step), step)
        return (
            pltpu.make_async_copy(weight.at[cut, :], w_buf.at[cut, :], load_sem.at[k]),
            pltpu.make_async_copy(
                features.at[:, :, cut], f_buf.at[:, :, cut], load_sem.at[parts + k]
            ),
        )

    for k in range(parts):
        for load in loads(k):
            load.start()

    quarters = cols // LANES

    def quarter(q):
        return pl.ds(pl.multiple_of((q % quarters) * LANES, LANES), LANES)

    def feature_cut(a):
        return pl.ds(pl.multiple_of(a * cols + (z % quarters) * LANES, LANES), LANES)

    own_k = pltpu.make_async_copy(
        features.at[c, :, feature_cut(i)], fk.at[c, i, :, quarter(z)], load_sem.at[2 * parts]
    )
    own_k.start()
    acc[...] = jnp.zeros_like(acc)

    pl.semaphore_wait(barrier, n_dp - 1 + ring - 1 + 1)
    feature_copies = []
    for d in range(1, n_dp):
        other = (i + d) % n_dp
        feature_copies.append(
            mail.push(
                features.at[c, :, feature_cut(other)], fk.at[c, i, :, quarter(z)], (other, j)
            )
        )

    def project(k, carry):
        for load in loads(k):
            load.wait()
        cut = pl.ds(pl.multiple_of(k * step, step), step)
        left = f_buf[:, :, cut].reshape(2 * rows, step)
        got = jnp.dot(left, w_buf[cut, :], preferred_element_type=jnp.float32)
        acc[:, 0:rows, :] += got.reshape(2, rows, cols)
        return carry

    lax.fori_loop(0, parts, project, 0)

    for v in range(2):
        turned[v] = acc[v].T
    strip_copies = []
    for d in range(1, n_dp):
        other = (i + d) % n_dp
        cut = pl.ds(pl.multiple_of(other * sub, sub), sub)
        strip_copies.append(mail.push(turned.at[:, cut, :], arrived.at[i], (other, j)))
    arrived[i] = turned[:, pl.ds(pl.multiple_of(i * sub, sub), sub), :]

    own_k.wait()
    for copy in feature_copies:
        copy.wait_recv()
    mine = fk.at[c, :, :, quarter(z)]
    feature_up = mail.push(mine, mine, zdev(up))
    feature_down = mail.push(mine, mine, zdev(down))

    for copy in strip_copies:
        copy.wait_recv()

    inv_std = [None, None]
    for v in (0, 1):
        strip = jnp.concatenate([arrived[a, v][:, 0:rows] for a in range(n_dp)], axis=1)
        mean = jnp.sum(strip, axis=1, keepdims=True) * scale
        shifted = strip - mean
        variance = jnp.sum(shifted * shifted, axis=1, keepdims=True) * scale
        inv_std[v] = lax.rsqrt(variance + epsilon)
        centered = shifted * inv_std[v]
        cent[v] = centered
        if v == 0:
            t0[j] = centered.astype(jnp.bfloat16)
        else:
            t1[i] = centered.astype(jnp.bfloat16)

    def gather(block, first_flip):
        own = block(index_of(q1, q2))
        ends = []

        def onward(a):
            part = block(index_of(a, q2))
            return (mail.push(part, part, ring2(right2)), mail.push(part, part, ring2(left2)))

        def across(n, a, pair):
            pair[0].wait_recv()
            pair[1].wait_recv()
            if (n + first_flip) % 2 == 0:
                part = block(index_of(a, left2))
                ends.append(mail.push(part, part, ring2(right2)))
            else:
                part = block(index_of(a, right2))
                ends.append(mail.push(part, part, ring2(left2)))

        to_right = mail.push(own, own, ring1(right1))
        to_left = mail.push(own, own, ring1(left1))
        pair_own = onward(q1)
        yield
        to_right.wait_recv()
        part = block(index_of(left1, q2)).at[low]
        far_low = mail.push(part, part, ring1(right1))
        pair_left = onward(left1)
        yield
        to_left.wait_recv()
        part = block(index_of(right1, q2)).at[high]
        far_high = mail.push(part, part, ring1(left1))
        pair_right = onward(right1)
        yield
        across(0, q1, pair_own)
        yield
        far_low.wait_recv()
        far_high.wait_recv()
        pair_far = onward(far1)
        yield
        across(1, left1, pair_left)
        yield
        across(2, right1, pair_right)
        yield
        across(3, far1, pair_far)
        yield
        for copy in ends:
            copy.wait_recv()

    def gather_z():
        side = []

        def to_side(q):
            part = t0.at[q * CORES + c]
            side.append(mail.push(part, part, sibling))

        part = t0.at[j]
        ups, downs = [mail.push(part, part, zdev(up))], [mail.push(part, part, zdev(down))]
        to_side(z)
        for t in range(1, far):
            yield
            below, above = (z + ring - t) % ring, (z + t) % ring
            part = t0.at[below * CORES + c]
            ups[-1].wait_recv()
            part = part if t < far - 1 else part.at[low]
            ups.append(mail.push(part, part, zdev(up)))
            part = t0.at[above * CORES + c]
            downs[-1].wait_recv()
            part = part if t < far - 1 else part.at[high]
            downs.append(mail.push(part, part, zdev(down)))
            to_side(below)
            to_side(above)
        yield
        ups[-1].wait_recv()
        downs[-1].wait_recv()
        to_side((z + far) % ring)
        yield
        for copy in side:
            copy.wait_recv()

    def feature_chain():
        yield
        feature_up.wait_recv()
        part = fk.at[c, pl.ds(0, n_dp // 2), :, quarter(z + ring - 1)]
        one = mail.push(part, part, zdev(up))
        feature_down.wait_recv()
        part = fk.at[c, pl.ds(n_dp // 2, n_dp // 2), :, quarter(z + 1)]
        two = mail.push(part, part, zdev(down))
        yield
        one.wait_recv()
        two.wait_recv()
        last = mail.push(fk.at[c], fk.at[c], sibling)
        yield
        last.wait_recv()

    def run(chain, steps=99):
        for _ in range(steps):
            if next(chain, 0) == 0:
                return

    rows_of_second = gather(lambda a: t1.at[a], 0)
    rows_of_first = gather_z()
    wanted = feature_chain()
    run(rows_of_second, 1)
    run(rows_of_first, 1)
    run(wanted, 1)
    run(rows_of_second, 2)
    run(rows_of_first, 1)
    run(rows_of_second, 1)
    run(rows_of_first, 1)
    run(wanted, 1)
    run(rows_of_second, 2)
    run(rows_of_first, 1)
    run(rows_of_second, 2)
    run(rows_of_first, 1)
    run(wanted, 1)
    run(rows_of_first)
    run(rows_of_second)

    tile = 256

    def correlate(t, total):
        per = tile // sub
        left = t0[pl.ds(t * per, per)].reshape(tile, batch)
        corr = lax.dot_general(
            left, t1[...].reshape(cols, batch), (((1,), (1,)), ((), ())),
            preferred_element_type=jnp.float32,
        ) * scale
        r = t * tile + lax.broadcasted_iota(jnp.int32, (tile, cols), 0)
        where_diagonal = jnp.where(r // sub == j, i * sub + r % sub, -1)
        on_diagonal = where_diagonal == lax.broadcasted_iota(jnp.int32, (tile, cols), 1)
        gap = corr - 1.0
        terms = jnp.where(on_diagonal, gap * gap, off_weight * corr * corr)
        g = jnp.where(on_diagonal, 2.0 * gap, 2.0 * off_weight * corr)
        g_buf[pl.ds(pl.multiple_of(t * tile, tile), tile), :] = g.astype(jnp.bfloat16)
        gt_buf[:, pl.ds(pl.multiple_of(t * tile, tile), tile)] = g.T.astype(jnp.bfloat16)
        return total + jnp.sum(terms, axis=0, keepdims=True)

    total = lax.fori_loop(0, cols // tile, correlate, jnp.zeros((1, cols), jnp.float32))

    wide = batch // 3

    def partial(into, left, right):
        def one(t, carry):
            cut = pl.ds(pl.multiple_of(t * wide, wide), wide)
            got = jnp.dot(
                left[...], right[:, :, cut].reshape(cols, wide), preferred_element_type=jnp.float32
            )
            into[:, :, cut] = (got * scale).reshape(n_dp, sub, wide)
            return carry

        lax.fori_loop(0, batch // wide, one, 0)

    def scatter():
        fars_r = [mail.push(p1.at[index_of(far1, n)], opp_l.at[n], ring1(right1)) for n in (0, 1)]
        fars_l = [
            mail.push(p1.at[index_of(far1, 2 + n)], opp_r.at[n], ring1(left1)) for n in (0, 1)
        ]
        near_r = [None, None] + [
            mail.push(p1.at[index_of(right1, n)], fin_l.at[n], ring1(right1)) for n in (2, 3)
        ]
        near_l = [
            mail.push(p1.at[index_of(left1, n)], fin_r.at[n], ring1(left1)) for n in (0, 1)
        ] + [None, None]
        for n in (0, 1):
            yield
            fars_r[n].wait_recv()
            at = index_of(right1, n)
            p1[at] = p1[at] + opp_l[n]
            near_r[n] = mail.push(p1.at[at], fin_l.at[n], ring1(right1))
            fars_l[n].wait_recv()
            at = index_of(left1, 2 + n)
            p1[at] = p1[at] + opp_r[n]
            near_l[2 + n] = mail.push(p1.at[at], fin_r.at[2 + n], ring1(left1))
        yield
        for n in range(SIDE):
            near_r[n].wait_recv()
            near_l[n].wait_recv()
            at = index_of(q1, n)
            p1[at] = p1[at] + fin_l[n] + fin_r[n]
        at_far, at_right, at_left = (index_of(q1, q) for q in (far2, right2, left2))
        far_r = mail.push(p1.at[at_far, low], opp2_l, ring2(right2))
        far_l = mail.push(p1.at[at_far, high], opp2_r, ring2(left2))
        ends = [
            mail.push(p1.at[at_right, high], fin2_l.at[high], ring2(right2)),
            mail.push(p1.at[at_left, low], fin2_r.at[low], ring2(left2)),
        ]
        yield
        far_r.wait_recv()
        p1[at_right, low] = p1[at_right, low] + opp2_l[...]
        ends.append(mail.push(p1.at[at_right, low], fin2_l.at[low], ring2(right2)))
        far_l.wait_recv()
        p1[at_left, high] = p1[at_left, high] + opp2_r[...]
        ends.append(mail.push(p1.at[at_left, high], fin2_r.at[high], ring2(left2)))
        yield
        for copy in ends:
            copy.wait_recv()
        finish(1, p1[i] + fin2_l[...] + fin2_r[...])

    def scatter_z():
        order = [(z + far) % ring]
        for t in range(far - 1, 0, -1):
            order += [(z + t) % ring, (z + ring - t) % ring]
        order.append(z)
        side = [mail.push(p0.at[q * CORES + 1 - c], sib.at[q], sibling) for q in order]

        def settle(n):
            side[n].wait_recv()
            at = order[n] * CORES + c
            p0[at] = p0[at] + sib[order[n]]

        def above(t):
            return (z + t) % ring

        def below(t):
            return (z + ring - t) % ring

        def part(q, cut):
            return p0.at[q * CORES + c, cut]

        def pass_on(chain, buf, cut, dest, device):
            n = len(chain) - 1
            chain[n].wait_recv()
            at = dest * CORES + c
            p0[at, cut] = p0[at, cut] + buf[n]
            chain.append(mail.push(p0.at[at, cut], buf.at[n + 1], device))

        yield
        settle(0)
        ua = [mail.push(part(above(far), low), up_a.at[0], zdev(up))]
        db = [mail.push(part(below(far), high), down_b.at[0], zdev(down))]
        settle(1)
        ub = [mail.push(part(above(far - 1), high), up_b.at[0], zdev(up))]
        settle(2)
        da = [mail.push(part(below(far - 1), low), down_a.at[0], zdev(down))]
        for n in range(3, ring):
            settle(n)
        for t in range(far - 1, 0, -1):
            yield
            pass_on(ua, up_a, low, above(t), zdev(up))
            pass_on(db, down_b, high, below(t), zdev(down))
            if t > 1:
                yield
                pass_on(ub, up_b, high, above(t - 1), zdev(up))
                pass_on(da, down_a, low, below(t - 1), zdev(down))
        yield
        for chain in (ub, da, ua, db):
            chain[-1].wait_recv()
        p0[j, low] = p0[j, low] + up_a[far - 1] + down_a[far - 2]
        p0[j, high] = p0[j, high] + up_b[far - 2] + down_b[far - 1]
        finish(0, p0[j])

    def finish(v, got):
        first = jnp.sum(got, axis=1, keepdims=True) * scale
        cross = jnp.sum(got * cent[v], axis=1, keepdims=True) * scale
        og[v, i] = (inv_std[v] * (got - first - cent[v] * cross)).astype(jnp.bfloat16)

    def loss_chain(value):
        stages = (
            (loss_x, x, [(y * SIDE + (x + d) % SIDE, j) for d in range(1, SIDE)]),
            (loss_y, y, [(((y + d) % SIDE) * SIDE + x, j) for d in range(1, SIDE)]),
            (loss_z, z, [zdev((z + d) % ring) for d in range(1, ring)]),
            (loss_c, c, [sibling]),
        )
        for buf, at, others in stages:
            buf[at] = value
            copies = [mail.push(buf.at[at], buf.at[at], device) for device in others]
            yield
            for copy in copies:
                copy.wait_recv()
            value = buf[0]
            for n in range(1, buf.shape[0]):
                value = value + buf[n]
        loss[...] = value / (n_mp * cols)

    partial(p1, gt_buf, t0)
    second = scatter()
    run(second, 1)
    partial(p0, g_buf, t1)
    first = scatter_z()
    run(first, 1)
    score = loss_chain(jnp.broadcast_to(jnp.sum(total, axis=1, keepdims=True), (8, 128)))
    run(score, 1)
    run(first, 1)
    run(second, 2)
    run(first, 2)
    run(score, 1)
    run(first, 2)
    run(second, 1)
    run(first, 1)
    run(score, 1)
    run(second, 1)
    run(second)
    out_second = gather(lambda a: og.at[1, a], 1)
    run(out_second, 3)
    run(first)
    out_first = gather(lambda a: og.at[0, a], 0)
    run(out_first, 1)
    run(out_second, 2)
    run(out_first, 2)
    run(score, 1)
    run(out_second, 2)
    run(out_first, 2)
    run(out_second, 1)
    run(score)
    run(out_first, 3)
    run(out_second)
    run(out_first)
    run(wanted)

    half = cols // 2

    def weigh(t, carry):
        cut = pl.ds(pl.multiple_of(t * half, half), half)
        got = jnp.dot(
            og[0].reshape(cols, batch),
            fk[0, :, :, cut].reshape(batch, half),
            preferred_element_type=jnp.float32,
        ) + jnp.dot(
            og[1].reshape(cols, batch),
            fk[1, :, :, cut].reshape(batch, half),
            preferred_element_type=jnp.float32,
        )
        grad[cut, :] = got.T
        return carry

    lax.fori_loop(0, 2, weigh, 0)

    mail.close()


def body(n_dp, n_mp, features, weight):
    rows, depth = features.shape[1], features.shape[2]
    cols = weight.shape[1]
    batch = rows * n_dp
    sub = cols // n_dp
    ring = n_mp // CORES
    far = ring // 2
    f32, bf16 = jnp.float32, jnp.bfloat16
    V = pltpu.VMEM
    scratch = [
        V((depth, cols), bf16),
        V((2, rows, depth), bf16),
        V((2, LANES, cols), f32),
        V((2, cols, LANES), f32),
        V((n_dp, 2, sub, LANES), f32),
        V((2, sub, batch), f32),
        V((n_mp, sub, batch), bf16),
        V((n_dp, sub, batch), bf16),
        V((cols, cols), bf16),
        V((cols, cols), bf16),
        V((n_mp, sub, batch), f32),
        V((n_dp, sub, batch), f32),
        V((2, sub, batch), f32),
        V((2, sub, batch), f32),
        V((SIDE, sub, batch), f32),
        V((SIDE, sub, batch), f32),
        V((sub // 2, batch), f32),
        V((sub // 2, batch), f32),
        V((sub, batch), f32),
        V((sub, batch), f32),
        V((ring, sub, batch), f32),
        V((far, sub // 2, batch), f32),
        V((far - 1, sub // 2, batch), f32),
        V((far - 1, sub // 2, batch), f32),
        V((far, sub // 2, batch), f32),
        V((2, n_dp, sub, batch), bf16),
        V((2, n_dp, rows, cols), bf16),
        V((SIDE, 8, 128), f32),
        V((SIDE, 8, 128), f32),
        V((ring, 8, 128), f32),
        V((CORES, 8, 128), f32),
        pltpu.SemaphoreType.DMA((MSGS,)),
        pltpu.SemaphoreType.DMA((MSGS,)),
        pltpu.SemaphoreType.DMA((17,)),
    ]
    grad, loss = pl.pallas_call(
        functools.partial(kernel, n_dp, n_mp),
        out_shape=(
            jax.ShapeDtypeStruct((cols, cols), f32),
            jax.ShapeDtypeStruct((8, 128), f32),
        ),
        in_specs=[pl.BlockSpec(memory_space=pl.ANY)] * 2,
        out_specs=(pl.BlockSpec(memory_space=V), pl.BlockSpec(memory_space=V)),
        scratch_shapes=scratch,
        compiler_params=pltpu.CompilerParams(
            collective_id=0, has_side_effects=True, vmem_limit_bytes=60 * 2**20
        ),
    )(features, weight)
    return (grad, loss[0, 0])


def solution(mesh):
    placed = (P(None, "dp", None), P(None, "mp"))
    return jax.shard_map(
        functools.partial(body, mesh.shape["dp"], mesh.shape["mp"]),
        mesh=mesh,
        in_specs=placed,
        out_specs=(P("dp", "mp"), P()),
        check_vma=False,
    )
```

time: 514 us -> 104 us (0.20)
  waiting for transfers between devices: 251 us -> 0 us
  blocking collectives: 192 us -> 0 us
  Pallas kernels: 0 us -> 99 us
  matrix products: 32.7 us -> 0 us
  between operations: 15.6 us -> 0.64 us
  starting transfers between devices: 7.47 us -> 0 us
  local copies, waits for them, and re-layouts: 10.4 us -> 3.45 us
    psum x4 -> x0, blocking collectives: 192 us -> none  [the longest x1 77.8 us: body(): loss_value = lax.psum(jnp.sum(terms), ('dp', 'mp')) / full_width]
    all_gather x3 -> x0, waiting for transfers between devices: 160 us -> none  [the longest x1 75.7 us: body(): incoming = lax.all_gather(corr_grad, 'dp', axis=0, tiled=True)]
    pallas_call x0 -> x1, Pallas kernels: none -> 99 us  [body(): pl.pallas_call(functools.partial(kernel, n_dp, n_mp), out_shape=(jax.Shap...]
    reduce_scatter x2 -> x0, waiting for transfers between devices: 90.4 us -> none  [the longest x1 54.8 us: body(): lax.psum_scatter(across, 'mp', scatter_dimension=1, tiled=True) / batch_size]
    dot_general x5 -> x0, matrix products: 32.7 us -> none  [the longest x1 9.14 us: body(): jnp.einsum('vrk,vrc->kc', features, out_grad, preferred_element_type=jnp....]
    all_to_all x1 -> x0, starting transfers between devices: 7.27 us -> none  [body(): lax.all_to_all(first_full, 'dp', split_axis=1, concat_axis=0, tiled=True)]
    unnamed x8 -> x1, local copies, waits for them, and re-layouts: 7.7 us -> 2.26 us
  transfers between devices with their start and end apart: 6 -> 0, of which waited for: 5 -> 0; matrix products, arithmetic and copies ran while one was open for 2% -> 0% of each run, Pallas kernels for 0% -> 0%
where the time goes in v3:
time: 104 us; the launch traced here: 103 us
  Pallas kernels  99 us (95%)
  local copies, waits for them, and re-layouts  3.45 us (3%)
    pallas_call x1, Pallas kernels, body(): pl.pallas_call(functools.partial(kernel, n_dp, n_mp), out_shape=(jax.Shap...  99 us
    unnamed x1, local copies, waits for them, and re-layouts  2.26 us

profile of v3, /device:TPU:2, one launch (start us, length us, event | category | flops | bytes accessed | tf_op | source)
XLA Modules:
  0.0 103.0 jit_solution(1389653420494073771)
XLA Ops:
  0.6 99.0 %shard_map.41 = (f32[512,512]{1,0:T(8,128)}, f32[8,128]{1,0:T(8,128)}) custom-call(bf16[2,96,8192]{2,1,0:T(8,128)(2,1)} %features.1, bf16[8192,512]{1,0:T(8,128)(2,1)} %weight.1), custom_call_target="tpu_custom_call" | custom-call | tf_op jit(solution)/shard_map/pallas_call | solution.py:585
  99.6 1.2 %slice.3 = f32[1,1]{1,0:T(1,128)} slice(f32[8,128]{1,0:T(8,128)} %get-tuple-element.5), slice={[0:1], [0:1]} | slice | bytes 8 | tf_op jit(solution)/shard_map/slice | solution.py:598
  100.8 2.3 %copy.5 = f32[512,512]{1,0:T(8,128)} copy(f32[512,512]{1,0:T(8,128)} %get-tuple-element.8) | data formatting | bytes 2097152

commit v4 on v3

--- a/solution.py
+++ b/solution.py
@@ -12,7 +12,7 @@
 SIDE = 4
 CORES = 2
 LANES = 128
-MSGS = 160
+MSGS = 170
 MESH = pl.DeviceIdType.MESH
 
 
@@ -73,6 +73,7 @@
     down_b,
     og,
     fk,
+    part_buf,
     loss_x,
     loss_y,
     loss_z,
@@ -101,6 +102,9 @@
     def index_of(a, b):
         return a * s1 + b * s2
 
+    def slot_of(a, b):
+        return a * SIDE + b
+
     def ring1(q):
         return (index_of(q, q2), j)
 
@@ -140,29 +144,7 @@
         for load in loads(k):
             load.start()
 
-    quarters = cols // LANES
-
-    def quarter(q):
-        return pl.ds(pl.multiple_of((q % quarters) * LANES, LANES), LANES)
-
-    def feature_cut(a):
-        return pl.ds(pl.multiple_of(a * cols + (z % quarters) * LANES, LANES), LANES)
-
-    own_k = pltpu.make_async_copy(
-        features.at[c, :, feature_cut(i)], fk.at[c, i, :, quarter(z)], load_sem.at[2 * parts]
-    )
-    own_k.start()
     acc[...] = jnp.zeros_like(acc)
-
-    pl.semaphore_wait(barrier, n_dp - 1 + ring - 1 + 1)
-    feature_copies = []
-    for d in range(1, n_dp):
-        other = (i + d) % n_dp
-        feature_copies.append(
-            mail.push(
-                features.at[c, :, feature_cut(other)], fk.at[c, i, :, quarter(z)], (other, j)
-            )
-        )
 
     def project(k, carry):
         for load in loads(k):
@@ -174,22 +156,17 @@
         return carry
 
     lax.fori_loop(0, parts, project, 0)
-
     for v in range(2):
         turned[v] = acc[v].T
+
+    pl.semaphore_wait(barrier, n_dp - 1 + ring - 1 + 1)
+
     strip_copies = []
     for d in range(1, n_dp):
         other = (i + d) % n_dp
         cut = pl.ds(pl.multiple_of(other * sub, sub), sub)
         strip_copies.append(mail.push(turned.at[:, cut, :], arrived.at[i], (other, j)))
     arrived[i] = turned[:, pl.ds(pl.multiple_of(i * sub, sub), sub), :]
-
-    own_k.wait()
-    for copy in feature_copies:
-        copy.wait_recv()
-    mine = fk.at[c, :, :, quarter(z)]
-    feature_up = mail.push(mine, mine, zdev(up))
-    feature_down = mail.push(mine, mine, zdev(down))
 
     for copy in strip_copies:
         copy.wait_recv()
@@ -206,24 +183,24 @@
         if v == 0:
             t0[j] = centered.astype(jnp.bfloat16)
         else:
-            t1[i] = centered.astype(jnp.bfloat16)
-
-    def gather(block, first_flip):
-        own = block(index_of(q1, q2))
+            t1[slot_of(q1, q2)] = centered.astype(jnp.bfloat16)
+
+    def gather(block, at, first_flip):
+        own = block(at(q1, q2))
         ends = []
 
         def onward(a):
-            part = block(index_of(a, q2))
+            part = block(at(a, q2))
             return (mail.push(part, part, ring2(right2)), mail.push(part, part, ring2(left2)))
 
         def across(n, a, pair):
             pair[0].wait_recv()
             pair[1].wait_recv()
             if (n + first_flip) % 2 == 0:
-                part = block(index_of(a, left2))
+                part = block(at(a, left2))
                 ends.append(mail.push(part, part, ring2(right2)))
             else:
-                part = block(index_of(a, right2))
+                part = block(at(a, right2))
                 ends.append(mail.push(part, part, ring2(left2)))
 
         to_right = mail.push(own, own, ring1(right1))
@@ -231,12 +208,12 @@
         pair_own = onward(q1)
         yield
         to_right.wait_recv()
-        part = block(index_of(left1, q2)).at[low]
+        part = block(at(left1, q2)).at[low]
         far_low = mail.push(part, part, ring1(right1))
         pair_left = onward(left1)
         yield
         to_left.wait_recv()
-        part = block(index_of(right1, q2)).at[high]
+        part = block(at(right1, q2)).at[high]
         far_high = mail.push(part, part, ring1(left1))
         pair_right = onward(right1)
         yield
@@ -258,40 +235,76 @@
     def gather_z():
         side = []
 
+        def block(q):
+            return t0.at[q * CORES + c]
+
         def to_side(q):
-            part = t0.at[q * CORES + c]
-            side.append(mail.push(part, part, sibling))
-
-        part = t0.at[j]
-        ups, downs = [mail.push(part, part, zdev(up))], [mail.push(part, part, zdev(down))]
+            side.append(mail.push(block(q), block(q), sibling))
+
+        def hop(q, cut, device):
+            part = block(q).at[cut]
+            return mail.push(part, part, device)
+
+        up_low, down_high = hop(z, low, zdev(up)), hop(z, high, zdev(down))
+        up_high, down_low = hop(z, high, zdev(up)), hop(z, low, zdev(down))
         to_side(z)
         for t in range(1, far):
+            below, above = (z + ring - t) % ring, (z + t) % ring
             yield
-            below, above = (z + ring - t) % ring, (z + t) % ring
-            part = t0.at[below * CORES + c]
-            ups[-1].wait_recv()
-            part = part if t < far - 1 else part.at[low]
-            ups.append(mail.push(part, part, zdev(up)))
-            part = t0.at[above * CORES + c]
-            downs[-1].wait_recv()
-            part = part if t < far - 1 else part.at[high]
-            downs.append(mail.push(part, part, zdev(down)))
+            up_low.wait_recv()
+            up_low = hop(below, low, zdev(up))
+            down_high.wait_recv()
+            down_high = hop(above, high, zdev(down))
+            yield
+            up_high.wait_recv()
+            if t < far - 1:
+                up_high = hop(below, high, zdev(up))
+            down_low.wait_recv()
+            if t < far - 1:
+                down_low = hop(above, low, zdev(down))
             to_side(below)
             to_side(above)
         yield
-        ups[-1].wait_recv()
-        downs[-1].wait_recv()
+        up_low.wait_recv()
+        down_high.wait_recv()
         to_side((z + far) % ring)
         yield
         for copy in side:
             copy.wait_recv()
 
+    quarters = cols // LANES
+
+    def quarter(q):
+        return pl.ds(pl.multiple_of((q % quarters) * LANES, LANES), LANES)
+
+    def feature_cut(a):
+        return pl.ds(pl.multiple_of(a * cols + (z % quarters) * LANES, LANES), LANES)
+
     def feature_chain():
-        yield
-        feature_up.wait_recv()
+        own = pltpu.make_async_copy(
+            features.at[c, :, feature_cut(i)], fk.at[c, i, :, quarter(z)], load_sem.at[2 * parts]
+        )
+        own.start()
+        copies = []
+        for d in range(1, n_dp):
+            other = (i + d) % n_dp
+            copies.append(
+                mail.push(
+                    features.at[c, :, feature_cut(other)], fk.at[c, i, :, quarter(z)], (other, j)
+                )
+            )
+        yield
+        own.wait()
+        for copy in copies:
+            copy.wait_recv()
+        part = fk.at[c, :, :, quarter(z)]
+        one = mail.push(part, part, zdev(up))
+        two = mail.push(part, part, zdev(down))
+        yield
+        one.wait_recv()
         part = fk.at[c, pl.ds(0, n_dp // 2), :, quarter(z + ring - 1)]
         one = mail.push(part, part, zdev(up))
-        feature_down.wait_recv()
+        two.wait_recv()
         part = fk.at[c, pl.ds(n_dp // 2, n_dp // 2), :, quarter(z + 1)]
         two = mail.push(part, part, zdev(down))
         yield
@@ -306,24 +319,26 @@
             if next(chain, 0) == 0:
                 return
 
-    rows_of_second = gather(lambda a: t1.at[a], 0)
+    rows_of_second = gather(lambda a: t1.at[a], slot_of, 0)
     rows_of_first = gather_z()
     wanted = feature_chain()
     run(rows_of_second, 1)
     run(rows_of_first, 1)
-    run(wanted, 1)
     run(rows_of_second, 2)
     run(rows_of_first, 1)
     run(rows_of_second, 1)
     run(rows_of_first, 1)
+    run(rows_of_second, 1)
+    run(rows_of_first, 1)
+    run(rows_of_second, 1)
+    run(rows_of_first, 1)
+    run(rows_of_second, 1)
+    run(rows_of_first, 1)
+    run(rows_of_second, 1)
     run(wanted, 1)
-    run(rows_of_second, 2)
-    run(rows_of_first, 1)
-    run(rows_of_second, 2)
-    run(rows_of_first, 1)
-    run(wanted, 1)
+    run(rows_of_first, 2)
+    run(rows_of_second)
     run(rows_of_first)
-    run(rows_of_second)
 
     tile = 256
 
@@ -335,7 +350,7 @@
             preferred_element_type=jnp.float32,
         ) * scale
         r = t * tile + lax.broadcasted_iota(jnp.int32, (tile, cols), 0)
-        where_diagonal = jnp.where(r // sub == j, i * sub + r % sub, -1)
+        where_diagonal = jnp.where(r // sub == j, slot_of(q1, q2) * sub + r % sub, -1)
         on_diagonal = where_diagonal == lax.broadcasted_iota(jnp.int32, (tile, cols), 1)
         gap = corr - 1.0
         terms = jnp.where(on_diagonal, gap * gap, off_weight * corr * corr)
@@ -360,50 +375,57 @@
         lax.fori_loop(0, batch // wide, one, 0)
 
     def scatter():
-        fars_r = [mail.push(p1.at[index_of(far1, n)], opp_l.at[n], ring1(right1)) for n in (0, 1)]
-        fars_l = [
-            mail.push(p1.at[index_of(far1, 2 + n)], opp_r.at[n], ring1(left1)) for n in (0, 1)
-        ]
-        near_r = [None, None] + [
-            mail.push(p1.at[index_of(right1, n)], fin_l.at[n], ring1(right1)) for n in (2, 3)
-        ]
-        near_l = [
-            mail.push(p1.at[index_of(left1, n)], fin_r.at[n], ring1(left1)) for n in (0, 1)
-        ] + [None, None]
-        for n in (0, 1):
-            yield
-            fars_r[n].wait_recv()
-            at = index_of(right1, n)
-            p1[at] = p1[at] + opp_l[n]
-            near_r[n] = mail.push(p1.at[at], fin_l.at[n], ring1(right1))
-            fars_l[n].wait_recv()
-            at = index_of(left1, 2 + n)
-            p1[at] = p1[at] + opp_r[n]
-            near_l[2 + n] = mail.push(p1.at[at], fin_r.at[2 + n], ring1(left1))
-        yield
-        for n in range(SIDE):
-            near_r[n].wait_recv()
-            near_l[n].wait_recv()
-            at = index_of(q1, n)
-            p1[at] = p1[at] + fin_l[n] + fin_r[n]
-        at_far, at_right, at_left = (index_of(q1, q) for q in (far2, right2, left2))
-        far_r = mail.push(p1.at[at_far, low], opp2_l, ring2(right2))
-        far_l = mail.push(p1.at[at_far, high], opp2_r, ring2(left2))
-        ends = [
-            mail.push(p1.at[at_right, high], fin2_l.at[high], ring2(right2)),
-            mail.push(p1.at[at_left, low], fin2_r.at[low], ring2(left2)),
-        ]
-        yield
-        far_r.wait_recv()
+        f, r, l, o = far2, right2, left2, q2
+        far_f = mail.push(p1.at[slot_of(far1, f)], opp_l.at[0], ring1(right1))
+        far_l = mail.push(p1.at[slot_of(far1, l)], opp_r.at[0], ring1(left1))
+        far_r = mail.push(p1.at[slot_of(far1, r)], opp_l.at[1], ring1(right1))
+        far_o = mail.push(p1.at[slot_of(far1, o)], opp_r.at[1], ring1(left1))
+        l_right = mail.push(p1.at[slot_of(right1, l)], fin_l.at[2], ring1(right1))
+        f_left = mail.push(p1.at[slot_of(left1, f)], fin_r.at[0], ring1(left1))
+
+        def onward(copy, at, buf, n, into, m, device):
+            copy.wait_recv()
+            p1[at] = p1[at] + buf[n]
+            return mail.push(p1.at[at], into.at[m], device)
+
+        def settle(n, m, one, two):
+            one.wait_recv()
+            two.wait_recv()
+            at = slot_of(q1, n)
+            p1[at] = p1[at] + fin_l[m] + fin_r[m]
+            return at
+
+        yield
+        f_right = onward(far_f, slot_of(right1, f), opp_l, 0, fin_l, 0, ring1(right1))
+        l_left = onward(far_l, slot_of(left1, l), opp_r, 0, fin_r, 2, ring1(left1))
+        r_left = mail.push(p1.at[slot_of(left1, r)], fin_r.at[1], ring1(left1))
+        yield
+        r_right = onward(far_r, slot_of(right1, r), opp_l, 1, fin_l, 1, ring1(right1))
+        o_right = mail.push(p1.at[slot_of(right1, o)], fin_l.at[3], ring1(right1))
+        o_left = onward(far_o, slot_of(left1, o), opp_r, 1, fin_r, 3, ring1(left1))
+        yield
+        at = settle(f, 0, f_right, f_left)
+        opp_low = mail.push(p1.at[at, low], opp2_l, ring2(right2))
+        opp_high = mail.push(p1.at[at, high], opp2_r, ring2(left2))
+        yield
+        at_left = settle(l, 2, l_right, l_left)
+        ends = [mail.push(p1.at[at_left, low], fin2_r.at[low], ring2(left2))]
+        yield
+        at_right = settle(r, 1, r_right, r_left)
+        ends.append(mail.push(p1.at[at_right, high], fin2_l.at[high], ring2(right2)))
+        yield
+        opp_low.wait_recv()
         p1[at_right, low] = p1[at_right, low] + opp2_l[...]
         ends.append(mail.push(p1.at[at_right, low], fin2_l.at[low], ring2(right2)))
-        far_l.wait_recv()
+        opp_high.wait_recv()
         p1[at_left, high] = p1[at_left, high] + opp2_r[...]
         ends.append(mail.push(p1.at[at_left, high], fin2_r.at[high], ring2(left2)))
         yield
+        at = settle(o, 3, o_right, o_left)
+        yield
         for copy in ends:
             copy.wait_recv()
-        finish(1, p1[i] + fin2_l[...] + fin2_r[...])
+        finish(1, p1[at] + fin2_l[...] + fin2_r[...])
 
     def scatter_z():
         order = [(z + far) % ring]
@@ -479,7 +501,7 @@
             value = buf[0]
             for n in range(1, buf.shape[0]):
                 value = value + buf[n]
-        loss[...] = value / (n_mp * cols)
+        loss[...] = value[0:1, 0:1] / (n_mp * cols)
 
     partial(p1, gt_buf, t0)
     second = scatter()
@@ -489,50 +511,68 @@
     run(first, 1)
     score = loss_chain(jnp.broadcast_to(jnp.sum(total, axis=1, keepdims=True), (8, 128)))
     run(score, 1)
+    run(second, 1)
     run(first, 1)
-    run(second, 2)
-    run(first, 2)
-    run(score, 1)
-    run(first, 2)
     run(second, 1)
     run(first, 1)
     run(score, 1)
-    run(second, 1)
+    run(first, 1)
+    run(second, 1)
+    run(second, 1)
+    run(first, 1)
+    run(score, 1)
+    run(second, 1)
+    run(first, 1)
+    run(second, 1)
+    run(second, 1)
+    run(first, 1)
+    run(wanted, 1)
     run(second)
-    out_second = gather(lambda a: og.at[1, a], 1)
+    out_second = gather(lambda a: og.at[1, a], index_of, 1)
     run(out_second, 3)
+    run(score, 1)
     run(first)
-    out_first = gather(lambda a: og.at[0, a], 0)
+    out_first = gather(lambda a: og.at[0, a], index_of, 0)
     run(out_first, 1)
     run(out_second, 2)
     run(out_first, 2)
-    run(score, 1)
-    run(out_second, 2)
-    run(out_first, 2)
+    run(wanted, 1)
+    run(score)
     run(out_second, 1)
-    run(score)
-    run(out_first, 3)
+    run(out_first, 1)
+    run(out_second, 1)
+    run(out_first, 1)
+    run(out_second, 1)
+    run(out_first, 1)
+    run(wanted, 1)
+    run(out_first, 1)
+    run(out_first, 1)
     run(out_second)
-    run(out_first)
     run(wanted)
 
     half = cols // 2
 
-    def weigh(t, carry):
+    def weigh(v, t):
         cut = pl.ds(pl.multiple_of(t * half, half), half)
-        got = jnp.dot(
-            og[0].reshape(cols, batch),
-            fk[0, :, :, cut].reshape(batch, half),
-            preferred_element_type=jnp.float32,
-        ) + jnp.dot(
-            og[1].reshape(cols, batch),
-            fk[1, :, :, cut].reshape(batch, half),
+        return cut, jnp.dot(
+            og[v].reshape(cols, batch),
+            fk[v, :, :, cut].reshape(batch, half),
             preferred_element_type=jnp.float32,
         )
-        grad[cut, :] = got.T
+
+    def weigh_second(t, carry):
+        cut, got = weigh(1, t)
+        part_buf[:, cut] = got
         return carry
 
-    lax.fori_loop(0, 2, weigh, 0)
+    def weigh_first(t, carry):
+        cut, got = weigh(0, t)
+        grad[cut, :] = (got + part_buf[:, cut]).T
+        return carry
+
+    lax.fori_loop(0, 2, weigh_second, 0)
+    run(out_first)
+    lax.fori_loop(0, 2, weigh_first, 0)
 
     mail.close()
 
@@ -574,6 +614,7 @@
         V((far, sub // 2, batch), f32),
         V((2, n_dp, sub, batch), bf16),
         V((2, n_dp, rows, cols), bf16),
+        V((cols, cols), f32),
         V((SIDE, 8, 128), f32),
         V((SIDE, 8, 128), f32),
         V((ring, 8, 128), f32),
@@ -586,7 +627,7 @@
         functools.partial(kernel, n_dp, n_mp),
         out_shape=(
             jax.ShapeDtypeStruct((cols, cols), f32),
-            jax.ShapeDtypeStruct((8, 128), f32),
+            jax.ShapeDtypeStruct((1, 1), f32),
         ),
         in_specs=[pl.BlockSpec(memory_space=pl.ANY)] * 2,
         out_specs=(pl.BlockSpec(memory_space=V), pl.BlockSpec(memory_space=V)),
@@ -595,7 +636,7 @@
             collective_id=0, has_side_effects=True, vmem_limit_bytes=60 * 2**20
         ),
     )(features, weight)
-    return (grad, loss[0, 0])
+    return (grad, loss.reshape(()))
 
 
 def solution(mesh):

time: 104 us -> 97.9 us (0.941)
  Pallas kernels: 99 us -> 93.2 us
  between operations: 0.64 us -> 2.33 us
  local copies, waits for them, and re-layouts: 3.45 us -> 2.26 us
    pallas_call x1, Pallas kernels: 99 us -> 93.2 us  [body(): pl.pallas_call(functools.partial(kernel, n_dp, n_mp), out_shape=(jax.Shap...]
    slice x1 -> x0, local copies, waits for them, and re-layouts: 1.19 us -> none  [body(): return (grad, loss[0, 0])]
where the time goes in v4:
time: 97.9 us; the launch traced here: 97.8 us
  Pallas kernels  93.2 us (95%)
  between operations  2.33 us (2%)
  local copies, waits for them, and re-layouts  2.26 us (2%)
    pallas_call x1, Pallas kernels, body(): pl.pallas_call(functools.partial(kernel, n_dp, n_mp), out_shape=(jax.Shap...  93.2 us
    unnamed x1, local copies, waits for them, and re-layouts  2.26 us

profile of v4, /device:TPU:2, one launch (start us, length us, event | category | flops | bytes accessed | tf_op | source)
XLA Modules:
  0.0 97.8 jit_solution(17396041142840834697)
XLA Ops:
  0.6 93.2 %shard_map.41 = (f32[512,512]{1,0:T(8,128)}, f32[1,1]{1,0:T(1,128)}) custom-call(bf16[2,96,8192]{2,1,0:T(8,128)(2,1)} %features.1, bf16[8192,512]{1,0:T(8,128)(2,1)} %weight.1), custom_call_target="tpu_custom_call" | custom-call | tf_op jit(solution)/shard_map/pallas_call | solution.py:626
  93.8 2.3 %copy.6 = f32[512,512]{1,0:T(8,128)} copy(f32[512,512]{1,0:T(8,128)} %get-tuple-element.8) | data formatting | bytes 2097152

commit v5 on v4

--- a/solution.py
+++ b/solution.py
@@ -12,8 +12,12 @@
 SIDE = 4
 CORES = 2
 LANES = 128
-MSGS = 170
+MSGS = 190
 MESH = pl.DeviceIdType.MESH
+OFFSETS = sorted(
+    ((a, b) for a in range(SIDE) for b in range(SIDE) if a or b),
+    key=lambda o: -min(o[0], SIDE - o[0]) - min(o[1], SIDE - o[1]),
+)
 
 
 class Mail:
@@ -121,13 +125,6 @@
     mail = Mail(send_sem, recv_sem)
     low, high = pl.ds(0, sub // 2), pl.ds(sub // 2, sub // 2)
 
-    barrier = pltpu.get_barrier_semaphore()
-    for d in range(1, n_dp):
-        pl.semaphore_signal(barrier, inc=1, device_id=((i + d) % n_dp, j), device_id_type=MESH)
-    for d in range(1, ring):
-        pl.semaphore_signal(barrier, inc=1, device_id=zdev((z + d) % ring), device_id_type=MESH)
-    pl.semaphore_signal(barrier, inc=1, device_id=sibling, device_id_type=MESH)
-
     parts = 8
     step = depth // parts
 
@@ -144,6 +141,13 @@
         for load in loads(k):
             load.start()
 
+    barrier = pltpu.get_barrier_semaphore()
+    for d in range(1, n_dp):
+        pl.semaphore_signal(barrier, inc=1, device_id=((i + d) % n_dp, j), device_id_type=MESH)
+    for d in range(1, ring):
+        pl.semaphore_signal(barrier, inc=1, device_id=zdev((z + d) % ring), device_id_type=MESH)
+    pl.semaphore_signal(barrier, inc=1, device_id=sibling, device_id_type=MESH)
+
     acc[...] = jnp.zeros_like(acc)
 
     def project(k, carry):
@@ -161,18 +165,20 @@
 
     pl.semaphore_wait(barrier, n_dp - 1 + ring - 1 + 1)
 
-    strip_copies = []
-    for d in range(1, n_dp):
-        other = (i + d) % n_dp
-        cut = pl.ds(pl.multiple_of(other * sub, sub), sub)
-        strip_copies.append(mail.push(turned.at[:, cut, :], arrived.at[i], (other, j)))
+    strip_copies = ([], [])
+    for v in (0, 1):
+        for dx, dy in OFFSETS:
+            other = (y + dy) % SIDE * SIDE + (x + dx) % SIDE
+            cut = pl.ds(pl.multiple_of(other * sub, sub), sub)
+            strip_copies[v].append(
+                mail.push(turned.at[v, cut, :], arrived.at[i, v], (other, j))
+            )
     arrived[i] = turned[:, pl.ds(pl.multiple_of(i * sub, sub), sub), :]
-
-    for copy in strip_copies:
-        copy.wait_recv()
-
     inv_std = [None, None]
-    for v in (0, 1):
+
+    def normalize(v):
+        for copy in strip_copies[v]:
+            copy.wait_recv()
         strip = jnp.concatenate([arrived[a, v][:, 0:rows] for a in range(n_dp)], axis=1)
         mean = jnp.sum(strip, axis=1, keepdims=True) * scale
         shifted = strip - mean
@@ -180,10 +186,7 @@
         inv_std[v] = lax.rsqrt(variance + epsilon)
         centered = shifted * inv_std[v]
         cent[v] = centered
-        if v == 0:
-            t0[j] = centered.astype(jnp.bfloat16)
-        else:
-            t1[slot_of(q1, q2)] = centered.astype(jnp.bfloat16)
+        return centered.astype(jnp.bfloat16)
 
     def gather(block, at, first_flip):
         own = block(at(q1, q2))
@@ -205,22 +208,18 @@
 
         to_right = mail.push(own, own, ring1(right1))
         to_left = mail.push(own, own, ring1(left1))
+        to_far = mail.push(own, own, ring1(far1))
         pair_own = onward(q1)
         yield
         to_right.wait_recv()
-        part = block(at(left1, q2)).at[low]
-        far_low = mail.push(part, part, ring1(right1))
         pair_left = onward(left1)
         yield
         to_left.wait_recv()
-        part = block(at(right1, q2)).at[high]
-        far_high = mail.push(part, part, ring1(left1))
         pair_right = onward(right1)
         yield
         across(0, q1, pair_own)
         yield
-        far_low.wait_recv()
-        far_high.wait_recv()
+        to_far.wait_recv()
         pair_far = onward(far1)
         yield
         across(1, left1, pair_left)
@@ -286,8 +285,8 @@
         )
         own.start()
         copies = []
-        for d in range(1, n_dp):
-            other = (i + d) % n_dp
+        for dx, dy in OFFSETS:
+            other = (y + dy) % SIDE * SIDE + (x + dx) % SIDE
             copies.append(
                 mail.push(
                     features.at[c, :, feature_cut(other)], fk.at[c, i, :, quarter(z)], (other, j)
@@ -297,22 +296,36 @@
         own.wait()
         for copy in copies:
             copy.wait_recv()
-        part = fk.at[c, :, :, quarter(z)]
-        one = mail.push(part, part, zdev(up))
-        two = mail.push(part, part, zdev(down))
-        yield
-        one.wait_recv()
-        part = fk.at[c, pl.ds(0, n_dp // 2), :, quarter(z + ring - 1)]
-        one = mail.push(part, part, zdev(up))
-        two.wait_recv()
-        part = fk.at[c, pl.ds(n_dp // 2, n_dp // 2), :, quarter(z + 1)]
-        two = mail.push(part, part, zdev(down))
-        yield
-        one.wait_recv()
-        two.wait_recv()
-        last = mail.push(fk.at[c], fk.at[c], sibling)
-        yield
-        last.wait_recv()
+        halves = (pl.ds(0, n_dp // 2), pl.ds(n_dp // 2, n_dp // 2))
+
+        def send(n, q, device):
+            part = fk.at[c, halves[n], :, quarter(q)]
+            return mail.push(part, part, device)
+
+        def to_side(q):
+            part = fk.at[c, :, :, quarter(q)]
+            return mail.push(part, part, sibling)
+
+        ups = [send(0, z, zdev(up)), send(1, z, zdev(up))]
+        downs = [send(1, z, zdev(down)), send(0, z, zdev(down))]
+        side = [to_side(z)]
+        yield
+        ups[0].wait_recv()
+        ups.append(send(0, z + ring - 1, zdev(up)))
+        downs[0].wait_recv()
+        downs.append(send(1, z + 1, zdev(down)))
+        yield
+        ups[1].wait_recv()
+        side.append(to_side(z + ring - 1))
+        downs[1].wait_recv()
+        side.append(to_side(z + 1))
+        yield
+        ups[2].wait_recv()
+        downs[2].wait_recv()
+        side.append(to_side(z + 2))
+        yield
+        for copy in side:
+            copy.wait_recv()
 
     def run(chain, steps=99):
         for _ in range(steps):
@@ -322,7 +335,12 @@
     rows_of_second = gather(lambda a: t1.at[a], slot_of, 0)
     rows_of_first = gather_z()
     wanted = feature_chain()
+    t0[j] = normalize(0)
+    run(rows_of_first, 1)
+    t1[slot_of(q1, q2)] = normalize(1)
     run(rows_of_second, 1)
+    run(rows_of_first, 2)
+    run(rows_of_second, 2)
     run(rows_of_first, 1)
     run(rows_of_second, 2)
     run(rows_of_first, 1)
@@ -331,12 +349,8 @@
     run(rows_of_second, 1)
     run(rows_of_first, 1)
     run(rows_of_second, 1)
+    run(wanted, 1)
     run(rows_of_first, 1)
-    run(rows_of_second, 1)
-    run(rows_of_first, 1)
-    run(rows_of_second, 1)
-    run(wanted, 1)
-    run(rows_of_first, 2)
     run(rows_of_second)
     run(rows_of_first)
 
@@ -374,13 +388,23 @@
 
         lax.fori_loop(0, batch // wide, one, 0)
 
+    def partial_line(q):
+        cut = pl.ds(pl.multiple_of(q * (cols // SIDE), cols // SIDE), cols // SIDE)
+        got = jnp.dot(
+            gt_buf[cut, :], t0[...].reshape(cols, batch), preferred_element_type=jnp.float32
+        )
+        p1[pl.ds(q * SIDE, SIDE)] = (got * scale).reshape(SIDE, sub, batch)
+
     def scatter():
         f, r, l, o = far2, right2, left2, q2
+        partial_line(far1)
         far_f = mail.push(p1.at[slot_of(far1, f)], opp_l.at[0], ring1(right1))
         far_l = mail.push(p1.at[slot_of(far1, l)], opp_r.at[0], ring1(left1))
         far_r = mail.push(p1.at[slot_of(far1, r)], opp_l.at[1], ring1(right1))
         far_o = mail.push(p1.at[slot_of(far1, o)], opp_r.at[1], ring1(left1))
+        partial_line(right1)
         l_right = mail.push(p1.at[slot_of(right1, l)], fin_l.at[2], ring1(right1))
+        partial_line(left1)
         f_left = mail.push(p1.at[slot_of(left1, f)], fin_r.at[0], ring1(left1))
 
         def onward(copy, at, buf, n, into, m, device):
@@ -395,6 +419,7 @@
             p1[at] = p1[at] + fin_l[m] + fin_r[m]
             return at
 
+        partial_line(q1)
         yield
         f_right = onward(far_f, slot_of(right1, f), opp_l, 0, fin_l, 0, ring1(right1))
         l_left = onward(far_l, slot_of(left1, l), opp_r, 0, fin_r, 2, ring1(left1))
@@ -463,6 +488,7 @@
         ub = [mail.push(part(above(far - 1), high), up_b.at[0], zdev(up))]
         settle(2)
         da = [mail.push(part(below(far - 1), low), down_a.at[0], zdev(down))]
+        yield
         for n in range(3, ring):
             settle(n)
         for t in range(far - 1, 0, -1):
@@ -503,51 +529,46 @@
                 value = value + buf[n]
         loss[...] = value[0:1, 0:1] / (n_mp * cols)
 
-    partial(p1, gt_buf, t0)
     second = scatter()
     run(second, 1)
     partial(p0, g_buf, t1)
     first = scatter_z()
     run(first, 1)
     score = loss_chain(jnp.broadcast_to(jnp.sum(total, axis=1, keepdims=True), (8, 128)))
+    run(first, 1)
     run(score, 1)
     run(second, 1)
+    run(first, 2)
+    run(second, 1)
+    run(score, 1)
+    run(first, 2)
+    run(second, 2)
+    run(score, 1)
     run(first, 1)
     run(second, 1)
     run(first, 1)
-    run(score, 1)
-    run(first, 1)
-    run(second, 1)
-    run(second, 1)
-    run(first, 1)
-    run(score, 1)
-    run(second, 1)
-    run(first, 1)
-    run(second, 1)
-    run(second, 1)
-    run(first, 1)
     run(wanted, 1)
-    run(second)
-    out_second = gather(lambda a: og.at[1, a], index_of, 1)
-    run(out_second, 3)
+    run(second, 2)
     run(score, 1)
     run(first)
     out_first = gather(lambda a: og.at[0, a], index_of, 0)
     run(out_first, 1)
-    run(out_second, 2)
+    run(second)
+    out_second = gather(lambda a: og.at[1, a], index_of, 1)
+    run(out_second, 1)
     run(out_first, 2)
     run(wanted, 1)
     run(score)
-    run(out_second, 1)
-    run(out_first, 1)
-    run(out_second, 1)
-    run(out_first, 1)
-    run(out_second, 1)
+    run(out_second, 2)
+    run(out_first, 2)
+    run(out_second, 2)
+    run(wanted, 1)
+    run(out_first, 2)
+    run(out_second, 2)
     run(out_first, 1)
     run(wanted, 1)
-    run(out_first, 1)
-    run(out_first, 1)
-    run(out_second)
+    run(out_second, 1)
+    run(out_first)
     run(wanted)
 
     half = cols // 2
@@ -560,19 +581,19 @@
             preferred_element_type=jnp.float32,
         )
 
+    def weigh_first(t, carry):
+        cut, got = weigh(0, t)
+        part_buf[:, cut] = got
+        return carry
+
     def weigh_second(t, carry):
         cut, got = weigh(1, t)
-        part_buf[:, cut] = got
-        return carry
-
-    def weigh_first(t, carry):
-        cut, got = weigh(0, t)
         grad[cut, :] = (got + part_buf[:, cut]).T
         return carry
 
+    lax.fori_loop(0, 2, weigh_first, 0)
+    run(out_second)
     lax.fori_loop(0, 2, weigh_second, 0)
-    run(out_first)
-    lax.fori_loop(0, 2, weigh_first, 0)
 
     mail.close()
 

time: 97.9 us -> 94.1 us (0.961)
  Pallas kernels: 93.2 us -> 88.8 us
    pallas_call x1, Pallas kernels: 93.2 us -> 88.8 us  [body(): pl.pallas_call(functools.partial(kernel, n_dp, n_mp), out_shape=(jax.Shap...]
where the time goes in v5:
time: 94.1 us; the launch traced here: 93.4 us
  Pallas kernels  88.8 us (94%)
  between operations  2.33 us (2%)
  local copies, waits for them, and re-layouts  2.26 us (2%)
    pallas_call x1, Pallas kernels, body(): pl.pallas_call(functools.partial(kernel, n_dp, n_mp), out_shape=(jax.Shap...  88.8 us
    unnamed x1, local copies, waits for them, and re-layouts  2.26 us

profile of v5, /device:TPU:2, one launch (start us, length us, event | category | flops | bytes accessed | tf_op | source)
XLA Modules:
  0.0 93.4 jit_solution(5855220833447759423)
XLA Ops:
  0.6 88.8 %shard_map.41 = (f32[512,512]{1,0:T(8,128)}, f32[1,1]{1,0:T(1,128)}) custom-call(bf16[2,96,8192]{2,1,0:T(8,128)(2,1)} %features.1, bf16[8192,512]{1,0:T(8,128)(2,1)} %weight.1), custom_call_target="tpu_custom_call" | custom-call | tf_op jit(solution)/shard_map/pallas_call | solution.py:647
  89.4 2.3 %copy.6 = f32[512,512]{1,0:T(8,128)} copy(f32[512,512]{1,0:T(8,128)} %get-tuple-element.8) | data formatting | bytes 2097152

commit v6 on v5

--- a/solution.py
+++ b/solution.py
@@ -156,30 +156,106 @@
         cut = pl.ds(pl.multiple_of(k * step, step), step)
         left = f_buf[:, :, cut].reshape(2 * rows, step)
         got = jnp.dot(left, w_buf[cut, :], preferred_element_type=jnp.float32)
-        acc[:, 0:rows, :] += got.reshape(2, rows, cols)
+        acc[...] += got.reshape(2, rows, cols)
         return carry
 
     lax.fori_loop(0, parts, project, 0)
+    spare = LANES - rows
+    keep = sub * rows // LANES
+    tail = sub - keep
+    place = lax.broadcasted_iota(jnp.int32, (spare, cols), 1) % sub // tail
     for v in range(2):
-        turned[v] = acc[v].T
+        fill = jnp.zeros((spare, cols), jnp.float32)
+        for n in range(rows // spare):
+            moved = pltpu.roll(acc[v, n * spare : (n + 1) * spare, :], cols - keep + n * tail, 1)
+            fill = jnp.where(place == n, moved, fill)
+        turned[v] = jnp.concatenate([acc[v], fill], axis=0).T.reshape(n_dp, sub, LANES)
 
     pl.semaphore_wait(barrier, n_dp - 1 + ring - 1 + 1)
+
+    def run(chain, steps=99):
+        for _ in range(steps):
+            if next(chain, 0) == 0:
+                return
+
+    quarters = cols // LANES
+
+    def quarter(q):
+        return pl.ds(pl.multiple_of((q % quarters) * LANES, LANES), LANES)
+
+    def feature_cut(a):
+        return pl.ds(pl.multiple_of(a * cols + (z % quarters) * LANES, LANES), LANES)
+
+    def feature_chain():
+        own = pltpu.make_async_copy(
+            features.at[c, :, feature_cut(i)], fk.at[c, i, :, quarter(z)], load_sem.at[2 * parts]
+        )
+        own.start()
+        copies = []
+        for n, (dx, dy) in enumerate(OFFSETS):
+            other = (y + dy) % SIDE * SIDE + (x + dx) % SIDE
+            copies.append(
+                mail.push(
+                    features.at[c, :, feature_cut(other)], fk.at[c, i, :, quarter(z)], (other, j)
+                )
+            )
+        yield
+        own.wait()
+        for copy in copies:
+            copy.wait_recv()
+        halves = (pl.ds(0, n_dp // 2), pl.ds(n_dp // 2, n_dp // 2))
+
+        def send(n, q, device):
+            part = fk.at[c, halves[n], :, quarter(q)]
+            return mail.push(part, part, device)
+
+        def to_side(q):
+            part = fk.at[c, :, :, quarter(q)]
+            return mail.push(part, part, sibling)
+
+        ups = [send(0, z, zdev(up)), send(1, z, zdev(up))]
+        downs = [send(1, z, zdev(down)), send(0, z, zdev(down))]
+        side = [to_side(z)]
+        yield
+        ups[0].wait_recv()
+        ups.append(send(0, z + ring - 1, zdev(up)))
+        downs[0].wait_recv()
+        downs.append(send(1, z + 1, zdev(down)))
+        yield
+        ups[1].wait_recv()
+        side.append(to_side(z + ring - 1))
+        downs[1].wait_recv()
+        side.append(to_side(z + 1))
+        yield
+        ups[2].wait_recv()
+        downs[2].wait_recv()
+        side.append(to_side(z + 2))
+        yield
+        for copy in side:
+            copy.wait_recv()
+
+    wanted = feature_chain()
 
     strip_copies = ([], [])
     for v in (0, 1):
         for dx, dy in OFFSETS:
             other = (y + dy) % SIDE * SIDE + (x + dx) % SIDE
-            cut = pl.ds(pl.multiple_of(other * sub, sub), sub)
             strip_copies[v].append(
-                mail.push(turned.at[v, cut, :], arrived.at[i, v], (other, j))
+                mail.push(turned.at[v, other, pl.ds(0, keep)], arrived.at[v, i], (other, j))
             )
-    arrived[i] = turned[:, pl.ds(pl.multiple_of(i * sub, sub), sub), :]
+        arrived[v, i] = turned[v, i, 0:keep, :]
     inv_std = [None, None]
 
     def normalize(v):
         for copy in strip_copies[v]:
             copy.wait_recv()
-        strip = jnp.concatenate([arrived[a, v][:, 0:rows] for a in range(n_dp)], axis=1)
+        whole = jnp.concatenate([arrived[v, a][:, 0:rows] for a in range(n_dp)], axis=1)
+        parts = [
+            arrived[v, a][n * tail : (n + 1) * tail, rows:LANES]
+            for a in range(n_dp)
+            for n in range(rows // spare)
+        ]
+        strip = jnp.concatenate([whole, jnp.concatenate(parts, axis=1)], axis=0)
         mean = jnp.sum(strip, axis=1, keepdims=True) * scale
         shifted = strip - mean
         variance = jnp.sum(shifted * shifted, axis=1, keepdims=True) * scale
@@ -188,17 +264,21 @@
         cent[v] = centered
         return centered.astype(jnp.bfloat16)
 
-    def gather(block, at, first_flip):
+    def gather(block, at, first_flip, direct=False):
         own = block(at(q1, q2))
         ends = []
 
         def onward(a):
             part = block(at(a, q2))
+            if direct:
+                ends.append(mail.push(part, part, ring2(far2)))
             return (mail.push(part, part, ring2(right2)), mail.push(part, part, ring2(left2)))
 
         def across(n, a, pair):
             pair[0].wait_recv()
             pair[1].wait_recv()
+            if direct:
+                return
             if (n + first_flip) % 2 == 0:
                 part = block(at(a, left2))
                 ends.append(mail.push(part, part, ring2(right2)))
@@ -228,8 +308,10 @@
         yield
         across(3, far1, pair_far)
         yield
-        for copy in ends:
+        for copy in ends[:3]:
             copy.wait_recv()
+        yield
+        ends[3].wait_recv()
 
     def gather_z():
         side = []
@@ -271,70 +353,8 @@
         for copy in side:
             copy.wait_recv()
 
-    quarters = cols // LANES
-
-    def quarter(q):
-        return pl.ds(pl.multiple_of((q % quarters) * LANES, LANES), LANES)
-
-    def feature_cut(a):
-        return pl.ds(pl.multiple_of(a * cols + (z % quarters) * LANES, LANES), LANES)
-
-    def feature_chain():
-        own = pltpu.make_async_copy(
-            features.at[c, :, feature_cut(i)], fk.at[c, i, :, quarter(z)], load_sem.at[2 * parts]
-        )
-        own.start()
-        copies = []
-        for dx, dy in OFFSETS:
-            other = (y + dy) % SIDE * SIDE + (x + dx) % SIDE
-            copies.append(
-                mail.push(
-                    features.at[c, :, feature_cut(other)], fk.at[c, i, :, quarter(z)], (other, j)
-                )
-            )
-        yield
-        own.wait()
-        for copy in copies:
-            copy.wait_recv()
-        halves = (pl.ds(0, n_dp // 2), pl.ds(n_dp // 2, n_dp // 2))
-
-        def send(n, q, device):
-            part = fk.at[c, halves[n], :, quarter(q)]
-            return mail.push(part, part, device)
-
-        def to_side(q):
-            part = fk.at[c, :, :, quarter(q)]
-            return mail.push(part, part, sibling)
-
-        ups = [send(0, z, zdev(up)), send(1, z, zdev(up))]
-        downs = [send(1, z, zdev(down)), send(0, z, zdev(down))]
-        side = [to_side(z)]
-        yield
-        ups[0].wait_recv()
-        ups.append(send(0, z + ring - 1, zdev(up)))
-        downs[0].wait_recv()
-        downs.append(send(1, z + 1, zdev(down)))
-        yield
-        ups[1].wait_recv()
-        side.append(to_side(z + ring - 1))
-        downs[1].wait_recv()
-        side.append(to_side(z + 1))
-        yield
-        ups[2].wait_recv()
-        downs[2].wait_recv()
-        side.append(to_side(z + 2))
-        yield
-        for copy in side:
-            copy.wait_recv()
-
-    def run(chain, steps=99):
-        for _ in range(steps):
-            if next(chain, 0) == 0:
-                return
-
-    rows_of_second = gather(lambda a: t1.at[a], slot_of, 0)
+    rows_of_second = gather(lambda a: t1.at[a], slot_of, 0, direct=True)
     rows_of_first = gather_z()
-    wanted = feature_chain()
     t0[j] = normalize(0)
     run(rows_of_first, 1)
     t1[slot_of(q1, q2)] = normalize(1)
@@ -349,10 +369,10 @@
     run(rows_of_second, 1)
     run(rows_of_first, 1)
     run(rows_of_second, 1)
-    run(wanted, 1)
     run(rows_of_first, 1)
     run(rows_of_second)
     run(rows_of_first)
+    run(wanted, 1)
 
     tile = 256
 
@@ -402,6 +422,7 @@
         far_l = mail.push(p1.at[slot_of(far1, l)], opp_r.at[0], ring1(left1))
         far_r = mail.push(p1.at[slot_of(far1, r)], opp_l.at[1], ring1(right1))
         far_o = mail.push(p1.at[slot_of(far1, o)], opp_r.at[1], ring1(left1))
+        yield
         partial_line(right1)
         l_right = mail.push(p1.at[slot_of(right1, l)], fin_l.at[2], ring1(right1))
         partial_line(left1)
@@ -510,6 +531,34 @@
         first = jnp.sum(got, axis=1, keepdims=True) * scale
         cross = jnp.sum(got * cent[v], axis=1, keepdims=True) * scale
         og[v, i] = (inv_std[v] * (got - first - cent[v] * cross)).astype(jnp.bfloat16)
+
+    half = cols // 2
+
+    def weigh_first(t, carry):
+        cut = pl.ds(pl.multiple_of(t * half, half), half)
+        got = jnp.dot(
+            og[0].reshape(cols, batch),
+            fk[0, :, :, cut].reshape(batch, half),
+            preferred_element_type=jnp.float32,
+        )
+        part_buf[:, :, cut] = got.reshape(n_dp, sub, half)
+        return carry
+
+    def weigh(v, lines):
+        places = [index_of(q, n) for q in lines for n in range(SIDE)]
+
+        def one(t, carry):
+            cut = pl.ds(pl.multiple_of(t * half, half), half)
+            got = jnp.dot(
+                jnp.concatenate([og[v, a] for a in places], axis=0),
+                fk[v, :, :, cut].reshape(batch, half),
+                preferred_element_type=jnp.float32,
+            )
+            for n, a in enumerate(places):
+                part_buf[a, :, cut] += got[n * sub : (n + 1) * sub]
+            return carry
+
+        lax.fori_loop(0, 2, one, 0)
 
     def loss_chain(value):
         stages = (
@@ -535,65 +584,57 @@
     first = scatter_z()
     run(first, 1)
     score = loss_chain(jnp.broadcast_to(jnp.sum(total, axis=1, keepdims=True), (8, 128)))
+    run(second, 1)
     run(first, 1)
     run(score, 1)
     run(second, 1)
     run(first, 2)
     run(second, 1)
-    run(score, 1)
     run(first, 2)
-    run(second, 2)
-    run(score, 1)
+    run(second, 1)
     run(first, 1)
     run(second, 1)
     run(first, 1)
-    run(wanted, 1)
-    run(second, 2)
+    run(second, 1)
     run(score, 1)
+    run(second, 1)
     run(first)
     out_first = gather(lambda a: og.at[0, a], index_of, 0)
     run(out_first, 1)
     run(second)
     out_second = gather(lambda a: og.at[1, a], index_of, 1)
     run(out_second, 1)
-    run(out_first, 2)
-    run(wanted, 1)
-    run(score)
-    run(out_second, 2)
-    run(out_first, 2)
-    run(out_second, 2)
+    run(score, 1)
     run(wanted, 1)
     run(out_first, 2)
+    run(out_second, 1)
+    run(out_first, 2)
+    run(out_second, 1)
+    run(wanted, 1)
+    run(out_first, 1)
+    run(out_second, 2)
+    run(out_first, 1)
+    run(wanted, 1)
     run(out_second, 2)
     run(out_first, 1)
     run(wanted, 1)
     run(out_second, 1)
+    run(wanted)
+    run(score)
     run(out_first)
-    run(wanted)
-
-    half = cols // 2
-
-    def weigh(v, t):
+    lax.fori_loop(0, 2, weigh_first, 0)
+    run(out_second, 1)
+    weigh(1, (q1, left1, right1))
+
+    run(out_second)
+    weigh(1, (far1,))
+
+    def hand_over(t, carry):
         cut = pl.ds(pl.multiple_of(t * half, half), half)
-        return cut, jnp.dot(
-            og[v].reshape(cols, batch),
-            fk[v, :, :, cut].reshape(batch, half),
-            preferred_element_type=jnp.float32,
-        )
-
-    def weigh_first(t, carry):
-        cut, got = weigh(0, t)
-        part_buf[:, cut] = got
+        grad[cut, :] = part_buf[:, :, cut].reshape(cols, half).T
         return carry
 
-    def weigh_second(t, carry):
-        cut, got = weigh(1, t)
-        grad[cut, :] = (got + part_buf[:, cut]).T
-        return carry
-
-    lax.fori_loop(0, 2, weigh_first, 0)
-    run(out_second)
-    lax.fori_loop(0, 2, weigh_second, 0)
+    lax.fori_loop(0, 2, hand_over, 0)
 
     mail.close()
 
@@ -610,9 +651,9 @@
     scratch = [
         V((depth, cols), bf16),
         V((2, rows, depth), bf16),
-        V((2, LANES, cols), f32),
-        V((2, cols, LANES), f32),
-        V((n_dp, 2, sub, LANES), f32),
+        V((2, rows, cols), f32),
+        V((2, n_dp, sub, LANES), f32),
+        V((2, n_dp, sub * rows // LANES, LANES), f32),
         V((2, sub, batch), f32),
         V((n_mp, sub, batch), bf16),
         V((n_dp, sub, batch), bf16),
@@ -635,7 +676,7 @@
         V((far, sub // 2, batch), f32),
         V((2, n_dp, sub, batch), bf16),
         V((2, n_dp, rows, cols), bf16),
-        V((cols, cols), f32),
+        V((n_dp, sub, cols), f32),
         V((SIDE, 8, 128), f32),
         V((SIDE, 8, 128), f32),
         V((ring, 8, 128), f32),

time: 94.1 us -> 88.8 us (0.944)
  Pallas kernels: 88.8 us -> 83.8 us
    pallas_call x1, Pallas kernels: 88.8 us -> 83.8 us  [body(): pl.pallas_call(functools.partial(kernel, n_dp, n_mp), out_shape=(jax.Shap...]
where the time goes in v6:
time: 88.8 us; the launch traced here: 88.4 us
  Pallas kernels  83.8 us (94%)
  between operations  2.33 us (3%)
  local copies, waits for them, and re-layouts  2.26 us (3%)
    pallas_call x1, Pallas kernels, body(): pl.pallas_call(functools.partial(kernel, n_dp, n_mp), out_shape=(jax.Shap...  83.8 us
    unnamed x1, local copies, waits for them, and re-layouts  2.26 us

profile of v6, /device:TPU:2, one launch (start us, length us, event | category | flops | bytes accessed | tf_op | source)
XLA Modules:
  0.0 88.4 jit_solution(11045583418403948990)
XLA Ops:
  0.6 83.8 %shard_map.41 = (f32[512,512]{1,0:T(8,128)}, f32[1,1]{1,0:T(1,128)}) custom-call(bf16[2,96,8192]{2,1,0:T(8,128)(2,1)} %features.1, bf16[8192,512]{1,0:T(8,128)(2,1)} %weight.1), custom_call_target="tpu_custom_call" | custom-call | tf_op jit(solution)/shard_map/pallas_call | solution.py:688
  84.5 2.3 %copy.6 = f32[512,512]{1,0:T(8,128)} copy(f32[512,512]{1,0:T(8,128)} %get-tuple-element.8) | data formatting | bytes 2097152

commit v7 on v6

--- a/solution.py
+++ b/solution.py
@@ -13,6 +13,7 @@
 CORES = 2
 LANES = 128
 MSGS = 190
+WHOLE, HALF = 12, 20
 MESH = pl.DeviceIdType.MESH
 OFFSETS = sorted(
     ((a, b) for a in range(SIDE) for b in range(SIDE) if a or b),
@@ -62,19 +63,11 @@
     gt_buf,
     p0,
     p1,
-    opp_l,
-    opp_r,
-    fin_l,
-    fin_r,
-    opp2_l,
-    opp2_r,
-    fin2_l,
-    fin2_r,
+    whole_out,
+    whole_in,
+    half_out,
+    half_in,
     sib,
-    up_a,
-    up_b,
-    down_a,
-    down_b,
     og,
     fk,
     part_buf,
@@ -403,7 +396,9 @@
             got = jnp.dot(
                 left[...], right[:, :, cut].reshape(cols, wide), preferred_element_type=jnp.float32
             )
-            into[:, :, cut] = (got * scale).reshape(n_dp, sub, wide)
+            got = (got * scale).reshape(n_dp, sub // 8, 8, wide)
+            for n in range(wide // LANES):
+                into[:, :, t * (wide // LANES) + n] = got[..., n * LANES : (n + 1) * LANES]
             return carry
 
         lax.fori_loop(0, batch // wide, one, 0)
@@ -413,65 +408,104 @@
         got = jnp.dot(
             gt_buf[cut, :], t0[...].reshape(cols, batch), preferred_element_type=jnp.float32
         )
-        p1[pl.ds(q * SIDE, SIDE)] = (got * scale).reshape(SIDE, sub, batch)
+        got = (got * scale).reshape(SIDE, sub // 8, 8, batch)
+        for n in range(batch // LANES):
+            p1[pl.ds(q * SIDE, SIDE), :, n] = got[..., n * LANES : (n + 1) * LANES]
+
+    third = batch // LANES // 3
+    level = 32768.0
+
+    def pack(value):
+        groups = value.shape[0]
+        largest = jnp.max(jnp.max(jnp.abs(value), axis=1, keepdims=True), axis=3, keepdims=True)
+        largest = jnp.maximum(largest, 1e-30)
+        whole = jnp.floor(value * ((level - 2.0) / largest) + (level + 0.5))
+        one, two, three = (whole[:, n * third : (n + 1) * third] for n in range(3))
+        upper = jnp.floor(two * (1.0 / 256.0))
+        words = jnp.concatenate(
+            [one * 256.0 + upper, three * 256.0 + (two - upper * 256.0)], axis=1
+        ).reshape(groups * 2 * third, 8, LANES)
+        lane = lax.broadcasted_iota(jnp.int32, (8, LANES), 1)
+        steps = jnp.zeros((8, LANES), jnp.float32)
+        for n in range(groups):
+            steps = jnp.where(lane == n, largest[n, 0] * (1.0 / (level - 2.0)), steps)
+        return jnp.concatenate([words, steps[None]], axis=0)
+
+    def unpack(words, groups):
+        tiles = words[: groups * 2 * third].reshape(groups, 2 * third, 8, LANES)
+        first, second = tiles[:, :third], tiles[:, third:]
+        one, three = jnp.floor(first * (1.0 / 256.0)), jnp.floor(second * (1.0 / 256.0))
+        two = (first - one * 256.0) * 256.0 + (second - three * 256.0)
+        steps = words[groups * 2 * third]
+        step = jnp.stack([steps[:, n : n + 1] for n in range(groups)])[:, None]
+        return (jnp.concatenate([one, two, three], axis=1) - level) * step
+
+    used = {sub // 8: 0, sub // 16: 0}
+
+    def post(value, device):
+        groups = value.shape[0]
+        outs, ins = (whole_out, whole_in) if groups == sub // 8 else (half_out, half_in)
+        n = used[groups]
+        used[groups] += 1
+        outs[n] = pack(value)
+        return mail.push(outs.at[n], ins.at[n], device), ins, n, groups
+
+    def take(message):
+        copy, ins, n, groups = message
+        copy.wait_recv()
+        return unpack(ins[n], groups)
+
+    low_part, high_part = pl.ds(0, sub // 16), pl.ds(sub // 16, sub // 16)
 
     def scatter():
         f, r, l, o = far2, right2, left2, q2
         partial_line(far1)
-        far_f = mail.push(p1.at[slot_of(far1, f)], opp_l.at[0], ring1(right1))
-        far_l = mail.push(p1.at[slot_of(far1, l)], opp_r.at[0], ring1(left1))
-        far_r = mail.push(p1.at[slot_of(far1, r)], opp_l.at[1], ring1(right1))
-        far_o = mail.push(p1.at[slot_of(far1, o)], opp_r.at[1], ring1(left1))
+        far_f = post(p1[slot_of(far1, f)], ring1(right1))
+        far_l = post(p1[slot_of(far1, l)], ring1(left1))
+        far_r = post(p1[slot_of(far1, r)], ring1(right1))
+        far_o = post(p1[slot_of(far1, o)], ring1(left1))
         yield
         partial_line(right1)
-        l_right = mail.push(p1.at[slot_of(right1, l)], fin_l.at[2], ring1(right1))
+        l_right = post(p1[slot_of(right1, l)], ring1(right1))
         partial_line(left1)
-        f_left = mail.push(p1.at[slot_of(left1, f)], fin_r.at[0], ring1(left1))
-
-        def onward(copy, at, buf, n, into, m, device):
-            copy.wait_recv()
-            p1[at] = p1[at] + buf[n]
-            return mail.push(p1.at[at], into.at[m], device)
-
-        def settle(n, m, one, two):
-            one.wait_recv()
-            two.wait_recv()
+        f_left = post(p1[slot_of(left1, f)], ring1(left1))
+
+        def onward(message, at, device):
+            return post(p1[at] + take(message), device)
+
+        def settle(n, one, two):
             at = slot_of(q1, n)
-            p1[at] = p1[at] + fin_l[m] + fin_r[m]
+            p1[at] = p1[at] + take(one) + take(two)
             return at
 
         partial_line(q1)
         yield
-        f_right = onward(far_f, slot_of(right1, f), opp_l, 0, fin_l, 0, ring1(right1))
-        l_left = onward(far_l, slot_of(left1, l), opp_r, 0, fin_r, 2, ring1(left1))
-        r_left = mail.push(p1.at[slot_of(left1, r)], fin_r.at[1], ring1(left1))
-        yield
-        r_right = onward(far_r, slot_of(right1, r), opp_l, 1, fin_l, 1, ring1(right1))
-        o_right = mail.push(p1.at[slot_of(right1, o)], fin_l.at[3], ring1(right1))
-        o_left = onward(far_o, slot_of(left1, o), opp_r, 1, fin_r, 3, ring1(left1))
-        yield
-        at = settle(f, 0, f_right, f_left)
-        opp_low = mail.push(p1.at[at, low], opp2_l, ring2(right2))
-        opp_high = mail.push(p1.at[at, high], opp2_r, ring2(left2))
-        yield
-        at_left = settle(l, 2, l_right, l_left)
-        ends = [mail.push(p1.at[at_left, low], fin2_r.at[low], ring2(left2))]
-        yield
-        at_right = settle(r, 1, r_right, r_left)
-        ends.append(mail.push(p1.at[at_right, high], fin2_l.at[high], ring2(right2)))
-        yield
-        opp_low.wait_recv()
-        p1[at_right, low] = p1[at_right, low] + opp2_l[...]
-        ends.append(mail.push(p1.at[at_right, low], fin2_l.at[low], ring2(right2)))
-        opp_high.wait_recv()
-        p1[at_left, high] = p1[at_left, high] + opp2_r[...]
-        ends.append(mail.push(p1.at[at_left, high], fin2_r.at[high], ring2(left2)))
-        yield
-        at = settle(o, 3, o_right, o_left)
-        yield
-        for copy in ends:
-            copy.wait_recv()
-        finish(1, p1[at] + fin2_l[...] + fin2_r[...])
+        f_right = onward(far_f, slot_of(right1, f), ring1(right1))
+        l_left = onward(far_l, slot_of(left1, l), ring1(left1))
+        r_left = post(p1[slot_of(left1, r)], ring1(left1))
+        yield
+        r_right = onward(far_r, slot_of(right1, r), ring1(right1))
+        o_right = post(p1[slot_of(right1, o)], ring1(right1))
+        o_left = onward(far_o, slot_of(left1, o), ring1(left1))
+        yield
+        at = settle(f, f_right, f_left)
+        opp_low = post(p1[at, low_part], ring2(right2))
+        opp_high = post(p1[at, high_part], ring2(left2))
+        yield
+        at_left = settle(l, l_right, l_left)
+        lows = [post(p1[at_left, low_part], ring2(left2))]
+        yield
+        at_right = settle(r, r_right, r_left)
+        highs = [post(p1[at_right, high_part], ring2(right2))]
+        yield
+        lows.append(post(p1[at_right, low_part] + take(opp_low), ring2(right2)))
+        highs.append(post(p1[at_left, high_part] + take(opp_high), ring2(left2)))
+        yield
+        at = settle(o, o_right, o_left)
+        yield
+        total_low = p1[at, low_part] + take(lows[0]) + take(lows[1])
+        total_high = p1[at, high_part] + take(highs[0]) + take(highs[1])
+        finish(1, jnp.concatenate([total_low, total_high], axis=0))
 
     def scatter_z():
         order = [(z + far) % ring]
@@ -492,42 +526,45 @@
             return (z + ring - t) % ring
 
         def part(q, cut):
-            return p0.at[q * CORES + c, cut]
-
-        def pass_on(chain, buf, cut, dest, device):
-            n = len(chain) - 1
-            chain[n].wait_recv()
-            at = dest * CORES + c
-            p0[at, cut] = p0[at, cut] + buf[n]
-            chain.append(mail.push(p0.at[at, cut], buf.at[n + 1], device))
+            return p0[q * CORES + c, cut]
+
+        def pass_on(message, cut, dest, device):
+            return post(part(dest, cut) + take(message), device)
 
         yield
         settle(0)
-        ua = [mail.push(part(above(far), low), up_a.at[0], zdev(up))]
-        db = [mail.push(part(below(far), high), down_b.at[0], zdev(down))]
+        ua = post(part(above(far), low_part), zdev(up))
+        db = post(part(below(far), high_part), zdev(down))
         settle(1)
-        ub = [mail.push(part(above(far - 1), high), up_b.at[0], zdev(up))]
+        ub = post(part(above(far - 1), high_part), zdev(up))
         settle(2)
-        da = [mail.push(part(below(far - 1), low), down_a.at[0], zdev(down))]
+        da = post(part(below(far - 1), low_part), zdev(down))
         yield
         for n in range(3, ring):
             settle(n)
         for t in range(far - 1, 0, -1):
             yield
-            pass_on(ua, up_a, low, above(t), zdev(up))
-            pass_on(db, down_b, high, below(t), zdev(down))
+            ua = pass_on(ua, low_part, above(t), zdev(up))
+            db = pass_on(db, high_part, below(t), zdev(down))
             if t > 1:
                 yield
-                pass_on(ub, up_b, high, above(t - 1), zdev(up))
-                pass_on(da, down_a, low, below(t - 1), zdev(down))
-        yield
-        for chain in (ub, da, ua, db):
-            chain[-1].wait_recv()
-        p0[j, low] = p0[j, low] + up_a[far - 1] + down_a[far - 2]
-        p0[j, high] = p0[j, high] + up_b[far - 2] + down_b[far - 1]
-        finish(0, p0[j])
-
-    def finish(v, got):
+                ub = pass_on(ub, high_part, above(t - 1), zdev(up))
+                da = pass_on(da, low_part, below(t - 1), zdev(down))
+        yield
+        total_high = part(z, high_part) + take(ub)
+        total_low = part(z, low_part) + take(da)
+        total_low = total_low + take(ua)
+        total_high = total_high + take(db)
+        finish(0, jnp.concatenate([total_low, total_high], axis=0))
+
+    def finish(v, tiles):
+        got = jnp.concatenate(
+            [
+                jnp.concatenate([tiles[g, n] for n in range(batch // LANES)], axis=1)
+                for g in range(sub // 8)
+            ],
+            axis=0,
+        )
         first = jnp.sum(got, axis=1, keepdims=True) * scale
         cross = jnp.sum(got * cent[v], axis=1, keepdims=True) * scale
         og[v, i] = (inv_std[v] * (got - first - cent[v] * cross)).astype(jnp.bfloat16)
@@ -591,13 +628,12 @@
     run(first, 2)
     run(second, 1)
     run(first, 2)
-    run(second, 1)
+    run(second, 2)
     run(first, 1)
     run(second, 1)
     run(first, 1)
     run(second, 1)
     run(score, 1)
-    run(second, 1)
     run(first)
     out_first = gather(lambda a: og.at[0, a], index_of, 0)
     run(out_first, 1)
@@ -606,17 +642,13 @@
     run(out_second, 1)
     run(score, 1)
     run(wanted, 1)
-    run(out_first, 2)
-    run(out_second, 1)
-    run(out_first, 2)
-    run(out_second, 1)
-    run(wanted, 1)
-    run(out_first, 1)
+    run(out_first, 4)
     run(out_second, 2)
-    run(out_first, 1)
     run(wanted, 1)
     run(out_second, 2)
-    run(out_first, 1)
+    run(out_first, 3)
+    run(wanted, 1)
+    run(out_second, 2)
     run(wanted, 1)
     run(out_second, 1)
     run(wanted)
@@ -646,6 +678,7 @@
     sub = cols // n_dp
     ring = n_mp // CORES
     far = ring // 2
+    tiles = sub // 8 * (batch // LANES) * 2 // 3
     f32, bf16 = jnp.float32, jnp.bfloat16
     V = pltpu.VMEM
     scratch = [
@@ -659,21 +692,13 @@
         V((n_dp, sub, batch), bf16),
         V((cols, cols), bf16),
         V((cols, cols), bf16),
-        V((n_mp, sub, batch), f32),
-        V((n_dp, sub, batch), f32),
-        V((2, sub, batch), f32),
-        V((2, sub, batch), f32),
-        V((SIDE, sub, batch), f32),
-        V((SIDE, sub, batch), f32),
-        V((sub // 2, batch), f32),
-        V((sub // 2, batch), f32),
-        V((sub, batch), f32),
-        V((sub, batch), f32),
-        V((ring, sub, batch), f32),
-        V((far, sub // 2, batch), f32),
-        V((far - 1, sub // 2, batch), f32),
-        V((far - 1, sub // 2, batch), f32),
-        V((far, sub // 2, batch), f32),
+        V((n_mp, sub // 8, batch // LANES, 8, LANES), f32),
+        V((n_dp, sub // 8, batch // LANES, 8, LANES), f32),
+        V((WHOLE, tiles + 1, 8, LANES), f32),
+        V((WHOLE, tiles + 1, 8, LANES), f32),
+        V((HALF, tiles // 2 + 1, 8, LANES), f32),
+        V((HALF, tiles // 2 + 1, 8, LANES), f32),
+        V((ring, sub // 8, batch // LANES, 8, LANES), f32),
         V((2, n_dp, sub, batch), bf16),
         V((2, n_dp, rows, cols), bf16),
         V((n_dp, sub, cols), f32),

time: 88.8 us -> 86.5 us (0.974)
  Pallas kernels: 83.8 us -> 81.6 us
    pallas_call x1, Pallas kernels: 83.8 us -> 81.6 us  [body(): pl.pallas_call(functools.partial(kernel, n_dp, n_mp), out_shape=(jax.Shap...]
where the time goes in v7:
time: 86.5 us; the launch traced here: 86.2 us
  Pallas kernels  81.6 us (94%)
  between operations  2.33 us (3%)
  local copies, waits for them, and re-layouts  2.26 us (3%)
    pallas_call x1, Pallas kernels, body(): pl.pallas_call(functools.partial(kernel, n_dp, n_mp), out_shape=(jax.Shap...  81.6 us
    unnamed x1, local copies, waits for them, and re-layouts  2.26 us

profile of v7, /device:TPU:2, one launch (start us, length us, event | category | flops | bytes accessed | tf_op | source)
XLA Modules:
  0.0 86.2 jit_solution(7755148891970379677)
XLA Ops:
  0.6 81.6 %shard_map.41 = (f32[512,512]{1,0:T(8,128)}, f32[1,1]{1,0:T(1,128)}) custom-call(bf16[2,96,8192]{2,1,0:T(8,128)(2,1)} %features.1, bf16[8192,512]{1,0:T(8,128)(2,1)} %weight.1), custom_call_target="tpu_custom_call" | custom-call | tf_op jit(solution)/shard_map/pallas_call | solution.py:713
  82.3 2.3 %copy.6 = f32[512,512]{1,0:T(8,128)} copy(f32[512,512]{1,0:T(8,128)} %get-tuple-element.8) | data formatting | bytes 2097152

commit v8 on v7

--- a/solution.py
+++ b/solution.py
@@ -70,7 +70,6 @@
     sib,
     og,
     fk,
-    part_buf,
     loss_x,
     loss_y,
     loss_z,
@@ -257,43 +256,43 @@
         cent[v] = centered
         return centered.astype(jnp.bfloat16)
 
-    def gather(block, at, first_flip, direct=False):
+    def gather(block, at, first_flip, direct=()):
         own = block(at(q1, q2))
-        ends = []
-
-        def onward(a):
+        ends = {}
+
+        def onward(n, a):
             part = block(at(a, q2))
-            if direct:
-                ends.append(mail.push(part, part, ring2(far2)))
+            if n in direct:
+                ends[n] = mail.push(part, part, ring2(far2))
             return (mail.push(part, part, ring2(right2)), mail.push(part, part, ring2(left2)))
 
         def across(n, a, pair):
             pair[0].wait_recv()
             pair[1].wait_recv()
-            if direct:
+            if n in direct:
                 return
             if (n + first_flip) % 2 == 0:
                 part = block(at(a, left2))
-                ends.append(mail.push(part, part, ring2(right2)))
+                ends[n] = mail.push(part, part, ring2(right2))
             else:
                 part = block(at(a, right2))
-                ends.append(mail.push(part, part, ring2(left2)))
+                ends[n] = mail.push(part, part, ring2(left2))
 
         to_right = mail.push(own, own, ring1(right1))
         to_left = mail.push(own, own, ring1(left1))
         to_far = mail.push(own, own, ring1(far1))
-        pair_own = onward(q1)
+        pair_own = onward(0, q1)
         yield
         to_right.wait_recv()
-        pair_left = onward(left1)
+        pair_left = onward(1, left1)
         yield
         to_left.wait_recv()
-        pair_right = onward(right1)
+        pair_right = onward(2, right1)
         yield
         across(0, q1, pair_own)
         yield
         to_far.wait_recv()
-        pair_far = onward(far1)
+        pair_far = onward(3, far1)
         yield
         across(1, left1, pair_left)
         yield
@@ -301,8 +300,8 @@
         yield
         across(3, far1, pair_far)
         yield
-        for copy in ends[:3]:
-            copy.wait_recv()
+        for n in (0, 1, 2):
+            ends[n].wait_recv()
         yield
         ends[3].wait_recv()
 
@@ -346,7 +345,7 @@
         for copy in side:
             copy.wait_recv()
 
-    rows_of_second = gather(lambda a: t1.at[a], slot_of, 0, direct=True)
+    rows_of_second = gather(lambda a: t1.at[a], slot_of, 0, (0, 1, 2, 3))
     rows_of_first = gather_z()
     t0[j] = normalize(0)
     run(rows_of_first, 1)
@@ -360,9 +359,7 @@
     run(rows_of_second, 1)
     run(rows_of_first, 1)
     run(rows_of_second, 1)
-    run(rows_of_first, 1)
-    run(rows_of_second, 1)
-    run(rows_of_first, 1)
+    run(rows_of_first, 2)
     run(rows_of_second)
     run(rows_of_first)
     run(wanted, 1)
@@ -578,7 +575,7 @@
             fk[0, :, :, cut].reshape(batch, half),
             preferred_element_type=jnp.float32,
         )
-        part_buf[:, :, cut] = got.reshape(n_dp, sub, half)
+        grad[:, :, cut] = got.reshape(n_dp, sub, half)
         return carry
 
     def weigh(v, lines):
@@ -592,7 +589,7 @@
                 preferred_element_type=jnp.float32,
             )
             for n, a in enumerate(places):
-                part_buf[a, :, cut] += got[n * sub : (n + 1) * sub]
+                grad[a, :, cut] += got[n * sub : (n + 1) * sub]
             return carry
 
         lax.fori_loop(0, 2, one, 0)
@@ -637,19 +634,21 @@
     run(first)
     out_first = gather(lambda a: og.at[0, a], index_of, 0)
     run(out_first, 1)
+    run(wanted, 1)
     run(second)
     out_second = gather(lambda a: og.at[1, a], index_of, 1)
     run(out_second, 1)
     run(score, 1)
-    run(wanted, 1)
     run(out_first, 4)
     run(out_second, 2)
     run(wanted, 1)
     run(out_second, 2)
-    run(out_first, 3)
+    run(out_first, 2)
     run(wanted, 1)
-    run(out_second, 2)
+    run(out_first, 1)
+    run(out_second, 1)
     run(wanted, 1)
+    run(out_second, 1)
     run(out_second, 1)
     run(wanted)
     run(score)
@@ -660,13 +659,6 @@
 
     run(out_second)
     weigh(1, (far1,))
-
-    def hand_over(t, carry):
-        cut = pl.ds(pl.multiple_of(t * half, half), half)
-        grad[cut, :] = part_buf[:, :, cut].reshape(cols, half).T
-        return carry
-
-    lax.fori_loop(0, 2, hand_over, 0)
 
     mail.close()
 
@@ -701,7 +693,6 @@
         V((ring, sub // 8, batch // LANES, 8, LANES), f32),
         V((2, n_dp, sub, batch), bf16),
         V((2, n_dp, rows, cols), bf16),
-        V((n_dp, sub, cols), f32),
         V((SIDE, 8, 128), f32),
         V((SIDE, 8, 128), f32),
         V((ring, 8, 128), f32),
@@ -713,7 +704,7 @@
     grad, loss = pl.pallas_call(
         functools.partial(kernel, n_dp, n_mp),
         out_shape=(
-            jax.ShapeDtypeStruct((cols, cols), f32),
+            jax.ShapeDtypeStruct((n_dp, sub, cols), f32),
             jax.ShapeDtypeStruct((1, 1), f32),
         ),
         in_specs=[pl.BlockSpec(memory_space=pl.ANY)] * 2,
@@ -723,7 +714,7 @@
             collective_id=0, has_side_effects=True, vmem_limit_bytes=60 * 2**20
         ),
     )(features, weight)
-    return (grad, loss.reshape(()))
+    return (grad.reshape(cols, cols).T, loss.reshape(()))
 
 
 def solution(mesh):

time: 86.5 us -> 85.7 us (level)
  Pallas kernels: 81.6 us -> 80.4 us
    reshape x0 -> x1, local copies, waits for them, and re-layouts: none -> 2.53 us  [body(): return (grad.reshape(cols, cols).T, loss.reshape(()))]
    unnamed x1 -> x0, local copies, waits for them, and re-layouts: 2.26 us -> none
    pallas_call x1, Pallas kernels: 81.6 us -> 80.4 us  [body(): pl.pallas_call(functools.partial(kernel, n_dp, n_mp), out_shape=(jax.Shap...]
where the time goes in v8:
time: 85.7 us; the launch traced here: 85.3 us
  Pallas kernels  80.4 us (94%)
  local copies, waits for them, and re-layouts  2.53 us (3%)
  between operations  2.33 us (3%)
    pallas_call x1, Pallas kernels, body(): pl.pallas_call(functools.partial(kernel, n_dp, n_mp), out_shape=(jax.Shap...  80.4 us
    reshape x1, local copies, waits for them, and re-layouts, body(): return (grad.reshape(cols, cols).T, loss.reshape(()))  2.53 us

profile of v8, /device:TPU:2, one launch (start us, length us, event | category | flops | bytes accessed | tf_op | source)
XLA Modules:
  0.0 85.3 jit_solution(2690255812000539339)
XLA Ops:
  0.6 80.4 %shard_map.41 = (f32[16,32,512]{2,1,0:T(8,128)}, f32[1,1]{1,0:T(1,128)}) custom-call(bf16[2,96,8192]{2,1,0:T(8,128)(2,1)} %features.1, bf16[8192,512]{1,0:T(8,128)(2,1)} %weight.1), custom_call_target="tpu_custom_call" | custom-call | tf_op jit(solution)/shard_map/pallas_call | solution.py:704
  81.0 2.5 %copy.4 = f32[512,512]{0,1:T(8,128)} copy(f32[512,512]{1,0:T(8,128)} %bitcast.4) | data formatting | bytes 2097152 | tf_op jit(solution)/shard_map/reshape | solution.py:717

commit v9 on v8

--- a/solution.py
+++ b/solution.py
@@ -625,10 +625,11 @@
     run(first, 2)
     run(second, 1)
     run(first, 2)
-    run(second, 2)
+    run(second, 1)
     run(first, 1)
     run(second, 1)
     run(first, 1)
+    run(second, 1)
     run(second, 1)
     run(score, 1)
     run(first)

time: 85.7 us -> 86 us (level)
  no operation moved by 1% of the time
where the time goes in v9:
time: 86 us; the launch traced here: 85.2 us
  Pallas kernels  80.3 us (93%)
  local copies, waits for them, and re-layouts  2.53 us (3%)
  between operations  2.33 us (3%)
    pallas_call x1, Pallas kernels, body(): pl.pallas_call(functools.partial(kernel, n_dp, n_mp), out_shape=(jax.Shap...  80.3 us
    reshape x1, local copies, waits for them, and re-layouts, body(): return (grad.reshape(cols, cols).T, loss.reshape(()))  2.53 us

profile of v9, /device:TPU:2, one launch (start us, length us, event | category | flops | bytes accessed | tf_op | source)
XLA Modules:
  0.0 85.2 jit_solution(6705104464863361279)
XLA Ops:
  0.6 80.3 %shard_map.41 = (f32[16,32,512]{2,1,0:T(8,128)}, f32[1,1]{1,0:T(1,128)}) custom-call(bf16[2,96,8192]{2,1,0:T(8,128)(2,1)} %features.1, bf16[8192,512]{1,0:T(8,128)(2,1)} %weight.1), custom_call_target="tpu_custom_call" | custom-call | tf_op jit(solution)/shard_map/pallas_call | solution.py:705
  81.0 2.5 %copy.4 = f32[512,512]{0,1:T(8,128)} copy(f32[512,512]{1,0:T(8,128)} %bitcast.4) | data formatting | bytes 2097152 | tf_op jit(solution)/shard_map/reshape | solution.py:718
